TPU v7x, 128 devices: a whole 4x4x4 slice. The times are simulated.
128 devices in a mesh: seq: 32 (over y, x, z_lo), chan: 4 (over z_hi, core).
Axes of the slice: x: 4, y: 4, z: 4 (z_hi: 2, z_lo: 2; z = z_hi * 2 + z_lo), core: 2. Of those that a mesh axis runs over, the one named last changes fastest.
Arguments:
- query_act: bfloat16 [4096, 4096], P('seq', 'chan'), may hold values from -6 to 6
- key_act: bfloat16 [4096, 4096], P('seq', 'chan'), may hold values from -6 to 6
- value_act: bfloat16 [4096, 4096], P('seq', 'chan'), may hold values from -6 to 6
- residue: float32 [16, 4096], P(None, 'chan'), may hold values from -2 to 2
- decay_rate: float32 [16, 4096], P(None, 'chan'), may hold values from 0.00012207031 to 0.03
- out_weight: bfloat16 [8192, 4096], P(None, 'chan'), may hold values from -0.0625 to 0.0625
- grad_out: bfloat16 [4096, 8192], P('seq', 'chan'), may hold values from -12 to 12
Outputs:
- grad_query: bfloat16 [4096, 4096], P('seq', 'chan')
- grad_key: bfloat16 [4096, 4096], P('seq', 'chan')
- grad_value: bfloat16 [4096, 4096], P('seq', 'chan')
- grad_out_weight: float32 [8192, 4096], P('seq', 'chan')
- grad_residue: float32 [16, 4096], P(None, 'chan')
- grad_log_rate: float32 [16, 4096], P(None, 'chan')
All inputs are finite; a program needn't handle non-finite values.
Results may differ from a plain program's by a relative error of at most 0.015.
Values may be sent and summed in bfloat16 or wider, within the bound.
A program may use at most 192 MiB of HBM per device.

v0:
```python
import math

import jax
import jax.numpy as jnp
from jax import lax
from jax.sharding import PartitionSpec as P

highest = lax.Precision.HIGHEST


def radix_list(length):
    result = []
    remain = length
    while remain > 1:
        factor = 1
        for option in range(2, min(remain, 128) + 1):
            if remain % option == 0:
                factor = option
        if factor == 1:
            factor = remain
        result.append(factor)
        remain = remain // factor
    return result


def angle_table(row_count, col_count, modulus, direction):
    row_ids = jnp.arange(row_count, dtype=jnp.int32)[:, None]
    col_ids = jnp.arange(col_count, dtype=jnp.int32)[None, :]
    product = row_ids * col_ids % modulus
    angles = direction * 2.0 * math.pi / modulus * product.astype(jnp.float32)
    return (jnp.cos(angles), jnp.sin(angles))


def apply_table(matrix, values):
    if values.shape[2] == 1:
        return jnp.einsum("ft,at->af", matrix, values[:, :, 0], precision=highest)[:, :, None]
    return jnp.einsum("ft,atb->afb", matrix, values, precision=highest)


def rotate_by(real_part, imag_part, cos_vals, sin_vals):
    return (
        real_part * cos_vals - imag_part * sin_vals,
        real_part * sin_vals + imag_part * cos_vals,
    )


def contract(real_part, imag_part, factor, direction, before, trailing):
    cos_vals, sin_vals = angle_table(factor, factor, factor, direction)
    real_view = real_part.reshape(before, factor, trailing)
    imag_view = imag_part.reshape(before, factor, trailing)
    new_real = apply_table(cos_vals, real_view) - apply_table(sin_vals, imag_view)
    new_imag = apply_table(sin_vals, real_view) + apply_table(cos_vals, imag_view)
    return (new_real, new_imag)


def rotate(real_part, imag_part, factor, remain, direction, before, trailing):
    cos_vals, sin_vals = angle_table(factor, remain, factor * remain, direction)
    view_shape = (before, factor, remain, trailing)
    return rotate_by(
        real_part.reshape(view_shape),
        imag_part.reshape(view_shape),
        cos_vals[None, :, :, None],
        sin_vals[None, :, :, None],
    )


def transform(real_part, imag_part, direction):
    leading, length, trailing = real_part.shape
    factors = radix_list(length)
    finished = 1
    remain = length
    for factor in factors:
        remain = remain // factor
        real_part, imag_part = contract(
            real_part, imag_part, factor, direction, leading * finished, remain * trailing
        )
        if remain > 1:
            real_part, imag_part = rotate(
                real_part, imag_part, factor, remain, direction, leading * finished, trailing
            )
        finished = finished * factor
    return (
        real_part.reshape(leading, length, trailing),
        imag_part.reshape(leading, length, trailing),
    )


def untransform(real_part, imag_part, direction):
    leading, length, trailing = real_part.shape
    factors = radix_list(length)
    for position in reversed(range(len(factors))):
        factor = factors[position]
        finished = math.prod(factors[:position])
        remain = math.prod(factors[position + 1 :])
        if remain > 1:
            real_part, imag_part = rotate(
                real_part, imag_part, factor, remain, direction, leading * finished, trailing
            )
        real_part, imag_part = contract(
            real_part, imag_part, factor, direction, leading * finished, remain * trailing
        )
    return (
        real_part.reshape(leading, length, trailing),
        imag_part.reshape(leading, length, trailing),
    )


def twist_halves(signal, positions, length):
    phases = math.pi / length * positions.astype(jnp.float32)
    cos_vals = jnp.cos(phases)
    sin_vals = jnp.sin(phases)
    real_part = jnp.stack([signal, signal * cos_vals], axis=1)
    imag_part = jnp.stack([jnp.zeros_like(signal), -signal * sin_vals], axis=1)
    return (real_part, imag_part)


def combine(real_part, imag_part, positions, length):
    phases = math.pi / length * positions.astype(jnp.float32)
    cos_vals = jnp.cos(phases)
    sin_vals = jnp.sin(phases)
    merged = real_part[:, 0] + cos_vals * real_part[:, 1] - sin_vals * imag_part[:, 1]
    return merged * (0.5 / length)


def spectral_products(real_part, imag_part):
    input_real, kernel_real, cot_real = (real_part[0], real_part[1], real_part[2])
    input_imag, kernel_imag, cot_imag = (imag_part[0], imag_part[1], imag_part[2])
    conv_real = kernel_real * input_real - kernel_imag * input_imag
    conv_imag = kernel_real * input_imag + kernel_imag * input_real
    back_real = kernel_real * cot_real + kernel_imag * cot_imag
    back_imag = kernel_real * cot_imag - kernel_imag * cot_real
    filt_real = input_real * cot_real + input_imag * cot_imag
    filt_imag = input_real * cot_imag - input_imag * cot_real
    return (
        jnp.stack([conv_real, back_real, filt_real]),
        jnp.stack([conv_imag, back_imag, filt_imag]),
    )


def filter_basis(rates, places):
    return jnp.sqrt(rates) * jnp.exp(-rates * places)


def sequence_layout(conv_input, conv_cot, residue, decay_rate, seq_count, seq_place, length):
    tok_rows, chan_cols = conv_input.shape
    slab_rows = tok_rows // seq_count
    input_slab, cot_slab = (
        lax.all_to_all(conv_input[None], "seq", split_axis=1, concat_axis=0, tiled=True),
        lax.all_to_all(conv_cot[None], "seq", split_axis=1, concat_axis=0, tiled=True),
    )
    source_ids = jnp.arange(seq_count, dtype=jnp.int32)
    slab_ids = seq_place * slab_rows + jnp.arange(slab_rows, dtype=jnp.int32)
    positions = source_ids[:, None] * tok_rows + slab_ids[None, :]
    places = positions.astype(jnp.float32)[None, :, :, None]
    mode_basis = filter_basis(decay_rate[:, None, None, :], places)
    kernel = jnp.sum(residue[:, None, None, :] * mode_basis, axis=0)
    signal = jnp.stack([input_slab.astype(jnp.float32), kernel, cot_slab.astype(jnp.float32)])
    real_part, imag_part = twist_halves(signal, positions[:, :, None], length)
    real_part = real_part.reshape(6, seq_count, slab_rows * chan_cols)
    imag_part = imag_part.reshape(6, seq_count, slab_rows * chan_cols)
    real_part, imag_part = transform(real_part, imag_part, -1.0)
    phases = (
        -2.0
        * math.pi
        / length
        * (source_ids[:, None] * slab_ids[None, :] % length).astype(jnp.float32)
    )
    real_part, imag_part = rotate_by(
        real_part.reshape(6, seq_count, slab_rows, chan_cols),
        imag_part.reshape(6, seq_count, slab_rows, chan_cols),
        jnp.cos(phases)[None, :, :, None],
        jnp.sin(phases)[None, :, :, None],
    )
    real_part, imag_part = (
        lax.all_to_all(real_part, "seq", split_axis=1, concat_axis=2, tiled=True),
        lax.all_to_all(imag_part, "seq", split_axis=1, concat_axis=2, tiled=True),
    )
    real_part, imag_part = transform(
        real_part.reshape(6, tok_rows, chan_cols), imag_part.reshape(6, tok_rows, chan_cols), -1.0
    )
    real_part, imag_part = spectral_products(
        real_part.reshape(3, 2, tok_rows, chan_cols), imag_part.reshape(3, 2, tok_rows, chan_cols)
    )
    real_part, imag_part = untransform(
        real_part.reshape(6, tok_rows, chan_cols), imag_part.reshape(6, tok_rows, chan_cols), 1.0
    )
    local_ids = jnp.arange(tok_rows, dtype=jnp.int32)
    phases = 2.0 * math.pi / length * (seq_place * local_ids % length).astype(jnp.float32)
    real_part, imag_part = rotate_by(
        real_part, imag_part, jnp.cos(phases)[None, :, None], jnp.sin(phases)[None, :, None]
    )
    real_part, imag_part = (
        lax.all_to_all(
            real_part.reshape(6, 1, tok_rows, chan_cols),
            "seq",
            split_axis=2,
            concat_axis=1,
            tiled=True,
        ),
        lax.all_to_all(
            imag_part.reshape(6, 1, tok_rows, chan_cols),
            "seq",
            split_axis=2,
            concat_axis=1,
            tiled=True,
        ),
    )
    real_part, imag_part = untransform(
        real_part.reshape(6, seq_count, slab_rows * chan_cols),
        imag_part.reshape(6, seq_count, slab_rows * chan_cols),
        1.0,
    )
    results = combine(
        real_part.reshape(3, 2, seq_count, slab_rows, chan_cols),
        imag_part.reshape(3, 2, seq_count, slab_rows, chan_cols),
        positions[:, :, None],
        length,
    )
    weighted = results[2][None] * mode_basis
    plain_sum = jnp.sum(weighted, axis=(1, 2))
    ramp_sum = jnp.sum(weighted * (0.5 - decay_rate[:, None, None, :] * places), axis=(1, 2))
    plain_sum, ramp_sum = lax.psum((plain_sum, ramp_sum), "seq")
    returned = lax.all_to_all(
        results[:2].astype(jnp.bfloat16), "seq", split_axis=1, concat_axis=2, tiled=True
    ).reshape(2, tok_rows, chan_cols)
    grad_scale = float(length) ** (-0.5)
    return (returned[0], returned[1], plain_sum * grad_scale, residue * ramp_sum * grad_scale)


def per_device(query_act, key_act, value_act, residue, decay_rate, out_weight, grad_out):
    tok_rows = query_act.shape[0]
    seq_count = lax.axis_size("seq")
    seq_place = lax.axis_index("seq")
    length = tok_rows * seq_count
    grad_scale = float(length) ** (-0.5)
    gathered = lax.all_gather(grad_out, "chan", axis=1, tiled=True)
    grad_mixed = jnp.dot(gathered, out_weight, preferred_element_type=jnp.float32).astype(
        jnp.bfloat16
    )
    conv_input = (key_act.astype(jnp.float32) * value_act.astype(jnp.float32)).astype(jnp.bfloat16)
    conv_cot = (grad_mixed.astype(jnp.float32) * query_act.astype(jnp.float32)).astype(jnp.bfloat16)
    conv_out, grad_conv, grad_res, grad_log = sequence_layout(
        conv_input, conv_cot, residue, decay_rate, seq_count, seq_place, length
    )
    gated_act = (query_act.astype(jnp.float32) * conv_out.astype(jnp.float32)).astype(jnp.bfloat16)
    columns_all = lax.all_to_all(gathered, "seq", split_axis=1, concat_axis=0, tiled=True)
    grad_weight = (
        lax.dot_general(
            columns_all,
            lax.all_gather(gated_act, "seq", axis=0, tiled=True),
            (((0,), (0,)), ((), ())),
            preferred_element_type=jnp.float32,
        )
        * grad_scale
    )
    grad_query = (grad_mixed.astype(jnp.float32) * conv_out.astype(jnp.float32)).astype(
        jnp.bfloat16
    )
    grad_key = (grad_conv.astype(jnp.float32) * value_act.astype(jnp.float32)).astype(jnp.bfloat16)
    grad_value = (grad_conv.astype(jnp.float32) * key_act.astype(jnp.float32)).astype(jnp.bfloat16)
    return (grad_query, grad_key, grad_value, grad_weight, grad_res, grad_log)


def solution(mesh):
    return jax.shard_map(
        per_device,
        mesh=mesh,
        in_specs=(
            P("seq", "chan"),
            P("seq", "chan"),
            P("seq", "chan"),
            P(None, "chan"),
            P(None, "chan"),
            P(None, "chan"),
            P("seq", "chan"),
        ),
        out_specs=(
            P("seq", "chan"),
            P("seq", "chan"),
            P("seq", "chan"),
            P("seq", "chan"),
            P(None, "chan"),
            P(None, "chan"),
        ),
        check_vma=False,
    )
```

profile of v0, /device:TPU:0, one launch (start us, length us, event | category | flops | bytes accessed | tf_op | source)
XLA Modules:
  0.0 887.6 jit_solution(2254355422049306516)
XLA Ops:
  14.4 8.8 all-to-all-start
  25.0 17.3 %all-gather.3.cloned.1.call-done = bf16[128,8192]{0,1:T(8,128)(2,1)} async-done(((bf16[128,2048]{0,1:T(8,128)(2,1)}), bf16[128,8192]{0,1:T(8,128)(2,1)}) %all-gather.3.cloned.1.call-update) | async-done | bytes 2097168 | tf_op jit(solution)/shard_map/all_gather | solution.py:236
  42.4 8.8 fusion.12
  55.5 7.4 all-to-all-start.1
  64.6 8.0 all-to-all-done.1
  75.9 3.7 copy.157
  79.6 4.1 reshape.409
  83.7 4.8 fusion.66
  88.5 4.8 fusion.62
  96.8 3.9 reshape.410
  100.7 5.9 fusion.2
  106.7 5.3 reshape.411
  111.9 6.3 fusion.3
  118.2 5.4 reshape.412
  123.6 4.8 multiply_add_fusion
  128.4 42.9 %all_to_all.82 = f32[6,32,4,1024]{3,2,0,1:T(4,128)S(1)} all-to-all(f32[6,32,4,1024]{3,2,0,1:T(4,128)S(1)} %get-tuple-element.59), channel_id=1, replica_groups=mesh['seq'=32,'chan'=4] {'seq'}, dimensions={1} | all-to-all | bytes 6291456 | tf_op jit(solution)/shard_map/all_to_all | solution.py:175
  171.3 4.8 all-to-all-start.3
  182.0 6.9 fusion.33
  188.9 6.9 fusion.29
  195.8 20.2 %all-to-all-done.3 = f32[6,32,4,1024]{3,2,0,1:T(4,128)} async-done(((f32[6,32,4,1024]{3,2,0,1:T(4,128)}), f32[6,32,4,1024]{3,2,0,1:T(4,128)}, u32[]{:S(2)}, u32[]{:S(2)}) %all-to-all-start.3) | async-done | bytes 3145760 | tf_op jit(solution)/shard_map/all_to_all | solution.py:176
  216.0 4.5 copy.167
  220.5 3.4 reshape.414
  223.9 7.4 subtract_bitcast_fusion.1
  231.3 5.4 add_bitcast_fusion.1
  237.9 3.4 fusion.23
  247.2 5.0 add_bitcast_fusion
  252.2 5.6 copy.171
  257.8 6.0 all-to-all-start.4
  263.8 8.6 copy.173
  272.4 30.5 %all-to-all-done.4 = f32[6,1,128,1024]{3,1,0,2:T(1,128)S(1)} async-done(((f32[6,1,128,1024]{3,1,0,2:T(1,128)}), f32[6,1,128,1024]{3,1,0,2:T(1,128)S(1)}, u32[]{:S(2)}, u32[]{:S(2)}) %all-to-all-start.4) | async-done | bytes 3145760 | tf_op jit(solution)/shard_map/all_to_all | solution.py:193
  302.9 7.3 all-to-all-start.5
  313.0 3.4 reshape.418
  316.4 4.9 fusion.56
  321.3 4.7 fusion.60
  326.0 24.2 %all-to-all-done.5 = f32[6,1,128,1024]{3,1,0,2:T(1,128)} async-done(((f32[6,1,128,1024]{3,1,0,2:T(1,128)}), f32[6,1,128,1024]{3,1,0,2:T(1,128)}, u32[]{:S(2)}, u32[]{:S(2)}) %all-to-all-start.5) | async-done | bytes 3145760 | tf_op jit(solution)/shard_map/all_to_all | solution.py:200
  350.2 4.6 copy.174
  354.8 3.4 reshape.420
  358.2 5.9 fusion.5
  364.2 5.3 reshape.422
  369.4 6.0 fusion.4
  375.4 3.9 reshape.421
  383.9 6.2 all-to-all-start.6
  390.1 4.1 multiply_reduce_fusion
  394.3 6.6 all-to-all-done.6
  404.2 29.5 %all_to_all.83 = bf16[128,32,256]{0,2,1:T(8,128)(2,1)} all-to-all(bf16[128,32,256]{0,2,1:T(8,128)(2,1)S(1)} %bitcast.161), channel_id=1, replica_groups=mesh['seq'=32,'chan'=4] {'seq'}, dimensions={1} | all-to-all | bytes 4194304 | tf_op jit(solution)/shard_map/all_to_all | solution.py:246
  437.0 248.0 %all-reduce.4.cloned.1.call-done = (f32[16,1024]{1,0:T(8,128)}, f32[16,1024]{1,0:T(8,128)}) async-done(((f32[16,1024]{1,0:T(8,128)}, f32[16,1024]{1,0:T(8,128)}), (f32[16,1024]{1,0:T(8,128)}, f32[16,1024]{1,0:T(8,128)})) %all-reduce.4.cloned.1.call-update) | async-done | bytes 131088 | tf_op jit(solution)/shard_map/psum | solution.py:222
  690.0 183.8 %all-gather.5.cloned.1.call-done = bf16[4096,1024]{1,0:T(8,128)(2,1)} async-done(((bf16[128,1024]{1,0:T(8,128)(2,1)}), bf16[4096,1024]{1,0:T(8,128)(2,1)}) %all-gather.5.cloned.1.call-update) | async-done | bytes 8388624 | tf_op jit(solution)/shard_map/all_gather | solution.py:250
  873.8 5.7 fusion.11
  (97 shorter events, 54.9 us)
Async XLA Ops:
  7.2 16.1 %copy-start.10 = (f32[16,1024]{1,0:T(8,128)S(1)}, f32[16,1024]{1,0:T(8,128)}, u32[]{:S(2)}) copy-start(f32[16,1024]{1,0:T(8,128)} %param.11) | copy-start | bytes 196612
  7.2 16.1 %copy-start.11 = (f32[16,1024]{1,0:T(8,128)S(1)}, f32[16,1024]{1,0:T(8,128)}, u32[]{:S(2)}) copy-start(f32[16,1024]{1,0:T(8,128)} %param.10) | copy-start | bytes 196612
  7.2 35.2 %all-gather.3.cloned.1.call-start = ((), (), s32[]{:S(2)}) async-start(), calls=%async_computation.8 | async-start | bytes 2621440 | tf_op jit(solution)/shard_map/all_gather | solution.py:236
  14.4 41.1 %all-to-all-start = ((bf16[32,2,2048]{2,1,0:T(2,128)(2,1)}), bf16[32,2,2048]{2,1,0:T(2,128)(2,1)S(1)}, u32[]{:S(2)}, u32[]{:S(2)}) async-start(bf16[32,2,2048]{2,1,0:T(2,128)(2,1)} %reshape.435), calls=%async_computation | async-start | bytes 524288 | tf_op jit(solution)/shard_map/all_to_all | solution.py:148
  23.3 19.1 %copy-start.13 = (f32[16,1024]{1,0:T(8,128)}, f32[16,1024]{1,0:T(8,128)S(1)}, u32[]{:S(2)}) copy-start(f32[16,1024]{1,0:T(8,128)S(1)} %get-tuple-element.78) | copy-start | bytes 196612
  23.3 19.1 %copy-start.15 = (f32[16,1024]{1,0:T(8,128)}, f32[16,1024]{1,0:T(8,128)S(1)}, u32[]{:S(2)}) copy-start(f32[16,1024]{1,0:T(8,128)S(1)} %get-tuple-element.79) | copy-start | bytes 196612
  25.0 26.9 %copy-start.8 = (bf16[128,1024]{1,0:T(8,128)(2,1)S(1)}, bf16[128,1024]{1,0:T(8,128)(2,1)}, u32[]{:S(2)}) copy-start(bf16[128,1024]{1,0:T(8,128)(2,1)} %param.7) | copy-start | bytes 786436
  51.1 0.8 copy-start.5
  55.5 17.2 %all-to-all-start.1 = ((bf16[32,2,2048]{2,1,0:T(2,128)(2,1)}), bf16[32,2,2048]{2,1,0:T(2,128)(2,1)S(1)}, u32[]{:S(2)}, u32[]{:S(2)}) async-start(bf16[32,2,2048]{2,1,0:T(2,128)(2,1)} %reshape.433), calls=%async_computation.1 | async-start | bytes 524288 | tf_op jit(solution)/shard_map/all_to_all | solution.py:149
  88.5 4.8 copy-start.4
  118.2 5.4 copy-start.1
  171.3 44.7 %all-to-all-start.3 = ((f32[6,32,4,1024]{3,2,0,1:T(4,128)}), f32[6,32,4,1024]{3,2,0,1:T(4,128)}, u32[]{:S(2)}, u32[]{:S(2)}) async-start(f32[6,32,4,1024]{3,2,0,1:T(4,128)} %get-tuple-element.58), calls=%async_computation.3 | async-start | bytes 6291456 | tf_op jit(solution)/shard_map/all_to_all | solution.py:176
  223.9 7.4 copy-start
  257.8 45.1 %all-to-all-start.4 = ((f32[6,1,128,1024]{3,1,0,2:T(1,128)}), f32[6,1,128,1024]{3,1,0,2:T(1,128)S(1)}, u32[]{:S(2)}, u32[]{:S(2)}) async-start(f32[6,1,128,1024]{3,1,0,2:T(1,128)} %copy.171), calls=%async_computation.4 | async-start | bytes 6291456 | tf_op jit(solution)/shard_map/all_to_all | solution.py:193
  302.9 47.3 %all-to-all-start.5 = ((f32[6,1,128,1024]{3,1,0,2:T(1,128)}), f32[6,1,128,1024]{3,1,0,2:T(1,128)}, u32[]{:S(2)}, u32[]{:S(2)}) async-start(f32[6,1,128,1024]{3,1,0,2:T(1,128)} %copy.173), calls=%async_computation.5 | async-start | bytes 6291456 | tf_op jit(solution)/shard_map/all_to_all | solution.py:200
  379.3 1.9 copy-start.3
  382.5 7.6 copy-start.14
  382.5 7.6 copy-start.16
  383.9 17.0 %all-to-all-start.6 = ((bf16[2,32,4,1024]{3,2,0,1:T(4,128)(2,1)}), bf16[2,32,4,1024]{3,2,0,1:T(4,128)(2,1)S(1)}, u32[]{:S(2)}, u32[]{:S(2)}) async-start(bf16[2,32,4,1024]{3,2,0,1:T(4,128)(2,1)} %slice.103), calls=%async_computation.6 | async-start | bytes 1048576 | tf_op jit(solution)/shard_map/all_to_all | solution.py:223
  390.1 13.2 %copy-start.6 = (f32[128,1024]{1,0:T(8,128)S(1)}, f32[128,1024]{1,0:T(8,128)}, u32[]{:S(2)}) copy-start(f32[128,1024]{1,0:T(8,128)} %copy-done.5) | copy-start | bytes 1572868
  390.1 294.9 %all-reduce.4.cloned.1.call-start = ((), (), s32[]{:S(2)}) async-start(), calls=%async_computation.10 | async-start | bytes 262144 | tf_op jit(solution)/shard_map/psum | solution.py:222
  394.2 9.9 %copy-start.2 = (bf16[128,8192]{0,1:T(8,128)(2,1)S(1)}, bf16[128,8192]{0,1:T(8,128)(2,1)}, u32[]{:S(2)}) copy-start(bf16[128,8192]{0,1:T(8,128)(2,1)} %all-gather.3.cloned.1.call-done) | copy-start | bytes 6291460
  394.3 479.5 %all-gather.5.cloned.1.call-start = ((), (), s32[]{:S(2)}) async-start(), calls=%async_computation.9 | async-start | bytes 8650752 | tf_op jit(solution)/shard_map/all_gather | solution.py:250
  433.6 252.8 %copy-start.12 = (f32[16,1024]{1,0:T(8,128)S(1)}, f32[16,1024]{1,0:T(8,128)}, u32[]{:S(2)}) copy-start(f32[16,1024]{1,0:T(8,128)} %param.10) | copy-start | bytes 196612
  433.6 254.3 %copy-start.7 = (f32[1,32,4,1024]{3,2,0,1:T(4,128)S(1)}, f32[1,32,4,1024]{3,2,0,1:T(4,128)}, u32[]{:S(2)}) copy-start(f32[1,32,4,1024]{3,2,0,1:T(4,128)} %get-tuple-element.76) | copy-start | bytes 1572868
  433.6 254.5 %copy-start.9 = (bf16[128,1024]{1,0:T(8,128)(2,1)S(1)}, bf16[128,1024]{1,0:T(8,128)(2,1)}, u32[]{:S(2)}) copy-start(bf16[128,1024]{1,0:T(8,128)(2,1)} %param.9) | copy-start | bytes 786436
Sparse Core Ops, SparseCore 0:
  10.3 32.0 all-gather.2
  394.4 290.4 all-reduce.3
  686.7 187.0 all-gather.4
where the time goes:
time: 897 us; the launch traced here: 888 us
  waiting for transfers between devices  539 us (60%)
  matrix products  98.7 us (11%)
  local copies, waits for them, and re-layouts  94.4 us (11%)
  blocking collectives  72.4 us (8%)
  starting transfers between devices  40.5 us (5%)
  other arithmetic  28.5 us (3%)
  between operations  14.5 us (2%)
    psum x1, waiting for transfers between devices, sequence_layout(): plain_sum, ramp_sum = lax.psum((plain_sum, ramp_sum), 'seq')  248 us
    all_gather x1, waiting for transfers between devices, per_device(): lax.all_gather(gated_act, 'seq', axis=0, tiled=True)  184 us
    dot_general x16, matrix products, apply_table(): return jnp.einsum('ft,atb->afb', matrix, values, precision=highest)  84.2 us
    all_to_all x1, blocking collectives, sequence_layout(): lax.all_to_all(real_part, 'seq', split_axis=1, concat_axis=2, tiled=True)  42.9 us
    all_to_all x1, waiting for transfers between devices, sequence_layout(): lax.all_to_all(real_part.reshape(6, 1, tok_rows, chan_cols), 'seq', split...  30.5 us
    all_to_all x1, blocking collectives, per_device(): lax.all_to_all(gathered, 'seq', split_axis=1, concat_axis=0, tiled=True)  29.5 us
    all_to_all x1, waiting for transfers between devices, sequence_layout(): lax.all_to_all(imag_part.reshape(6, 1, tok_rows, chan_cols), 'seq', split...  24.2 us
    all_to_all x1, waiting for transfers between devices, sequence_layout(): lax.all_to_all(imag_part, 'seq', split_axis=1, concat_axis=2, tiled=True)  20.2 us
  transfers between devices with their start and end apart: 9, of which 8 were waited for; matrix products, arithmetic and copies ran while one was open for 9% of the time, Pallas kernels for 0%

commit v1 on v0

v1 whole, which is shorter than its diff:
```python
import jax
import jax.numpy as jnp
from jax import lax
from jax.experimental import pallas as pl
from jax.experimental.pallas import tpu as pltpu
from jax.sharding import PartitionSpec as P

MESH = pl.DeviceIdType.MESH
F32 = jnp.float32
BF16 = jnp.bfloat16
ROWS = 128
COLS = 1024
TILES = 8
MODES = 16
PLANE = 8
LAYERS = 4
PARTS = 4
DPART = 2048
PIECE = 256
CHUNKS = 4
WIDE = COLS // CHUNKS
DEPTH = 512


def rows8(index):
    return pl.ds(pl.multiple_of(index * 8, 8), 8)


def body(
    q_ref, k_ref, v_ref, g_ref, res_ref, rate_ref, w_ref,
    gq_ref, gk_ref, gv_ref, gw_ref, gr_ref, gl_ref,
    wv, xs, cs, ys, hb, al, rl, gall, gt, at, gat, gm, co,
    hs, hin, so, sin, yin, ms, min, yin2, to, tin,
    rs_send, rs_recv, own, wsem, ssem, rsem,
):
    s = lax.axis_index("seq")
    c = lax.axis_index("chan")
    y = s // PLANE
    p = s % PLANE
    sib = (c // 2) * 2 + (1 - c % 2)
    far = (c + 2) % PARTS
    farsib = (sib + 2) % PARTS
    grad_scale = float(ROWS * PLANE * LAYERS) ** -0.5
    counter = [0]
    sends = []

    def plane(k):
        return (y * PLANE + (p + k) % PLANE, c)

    def layer(k):
        return (((y + k) % LAYERS) * PLANE + p, c)

    def ids(count):
        counter[0] += count
        return counter[0] - count

    def send(src, dst, device, slot):
        copy = pltpu.make_async_remote_copy(
            src_ref=src, dst_ref=dst, send_sem=ssem.at[slot], recv_sem=rsem.at[slot],
            device_id=device, device_id_type=MESH,
        )
        copy.start()
        sends.append(copy)
        return copy

    order = (c, sib, far, farsib)
    wcopies = []
    for n, h in enumerate(order):
        part = pl.ds(pl.multiple_of(h * DPART, DPART), DPART)
        copy = pltpu.make_async_copy(w_ref.at[part], wv.at[part], wsem.at[n])
        copy.start()
        wcopies.append(copy)

    barrier = pltpu.get_barrier_semaphore()
    greeted = [plane(k) for k in range(1, PLANE)] + [layer(k) for k in range(1, LAYERS)]
    greeted += [(s, sib), (s, far)]
    for device in greeted:
        pl.semaphore_signal(barrier, inc=1, device_id=device, device_id_type=MESH)

    for i in range(TILES):
        lanes = slice(128 * i, 128 * (i + 1))
        rate = rate_ref[:, lanes]
        al[pl.ds(i, MODES, stride=8), :] = jnp.exp(-rate)
        rl[pl.ds(i, MODES, stride=8), :] = res_ref[:, lanes] * jnp.sqrt(rate)
        x = (k_ref[:, lanes].astype(F32) * v_ref[:, lanes].astype(F32)).astype(BF16)
        xs[pl.ds(i, ROWS, stride=8), :] = x.astype(F32)

    def decay(m):
        return al[m * 8 : (m + 1) * 8, :]

    zero = jnp.zeros((8, 128), F32)

    def ahead(t, h):
        for u in range(4):
            x = xs[rows8(t * 4 + u), :]
            h = tuple(decay(m) * h[m] + x for m in range(MODES))
        return h

    h = lax.fori_loop(0, ROWS // 4, ahead, (zero,) * MODES)
    for m in range(MODES):
        hs[pl.ds(m, TILES, stride=MODES), :] = h[m]

    pl.semaphore_wait(barrier, len(greeted))

    def tile(index, size):
        return pl.ds(pl.multiple_of(index * size, size), size)

    slot = ids(PLANE - 1)
    h_in = [
        send(hs.at[tile((p + k) % PLANE, 16)], hin.at[tile(p, 16)], plane(k), slot + k - 1)
        for k in range(1, PLANE)
    ]
    slot = ids(3)
    g_far = send(g_ref, gall.at[c], (s, far), slot)
    g_sib = send(g_ref, gall.at[c], (s, sib), slot + 1)
    g_fwd_slot = slot + 2
    hin[tile(p, 16), :] = hs[tile(p, 16), :]
    gall[c] = g_ref[...]

    for k in range(PLANE):
        gt[k] = g_ref[:, PIECE * k : PIECE * (k + 1)].T
    slot = ids(PLANE - 1)
    mine = pl.ds(pl.multiple_of(p * ROWS, ROWS), ROWS)
    a_in = [
        send(gt.at[(p + k) % PLANE], at.at[c, :, mine], plane(k), slot + k - 1)
        for k in range(1, PLANE)
    ]
    at[c, :, mine] = gt[p]

    def mix(n, first):
        h = order[n]
        wcopies[n].wait()

        def step(j, carry):
            cols = pl.ds(pl.multiple_of(j * DEPTH, DEPTH), DEPTH)
            deep = pl.ds(pl.multiple_of(h * DPART + j * DEPTH, DEPTH), DEPTH)
            gm[...] += jnp.dot(gall[h, :, cols], wv[deep, :], preferred_element_type=F32)
            return carry

        lax.fori_loop(0, DPART // DEPTH, step, 0)

    gm[...] = jnp.zeros_like(gm)
    mix(0, True)

    my_tile = pl.ds(pl.multiple_of(p * 128, 128), 128)
    rate = rate_ref[:, my_tile]
    step_w = jnp.exp(-float(ROWS) * rate)
    layer_w = jnp.exp(-float(ROWS * PLANE) * rate)
    for copy in h_in:
        copy.wait_recv()
    state = jnp.zeros((MODES, 128), F32)
    for b in range(PLANE):
        so[b * 16 : (b + 1) * 16, :] = state
        state = step_w * state + hin[b * 16 : (b + 1) * 16, :]
    yin[tile(y, 16), :] = state
    slot = ids(LAYERS - 1)
    y_in = [
        send(yin.at[tile(y, 16)], yin.at[tile(y, 16)], layer(k), slot + k - 1)
        for k in range(1, LAYERS)
    ]
    g_sib.wait_recv()
    mix(1, False)
    for copy in y_in:
        copy.wait_recv()
    before = jnp.zeros((MODES, 128), F32)
    for b in range(LAYERS):
        before = jnp.where(b < y, layer_w * before + yin[b * 16 : (b + 1) * 16, :], before)
    for b in range(PLANE):
        so[b * 16 : (b + 1) * 16, :] += before
        before = step_w * before
    slot = ids(PLANE - 1)
    s_in = [
        send(so.at[tile((p + k) % PLANE, 16)], sin.at[tile(p, 16)], plane(k), slot + k - 1)
        for k in range(1, PLANE)
    ]
    sin[tile(p, 16), :] = so[tile(p, 16), :]

    for copy in a_in:
        copy.wait_recv()
    slot = ids(3)
    a_far = send(at.at[c], at.at[c], (s, far), slot)
    a_sib = send(at.at[c], at.at[c], (s, sib), slot + 1)
    a_fwd_slot = slot + 2
    g_far.wait_recv()
    g_fwd = send(gall.at[far], gall.at[far], (s, sib), g_fwd_slot)

    for copy in s_in:
        copy.wait_recv()

    def forward(t, h):
        for u in range(2):
            at_row = t * 2 + u
            x = xs[rows8(at_row), :]
            h = tuple(decay(m) * h[m] + x for m in range(MODES))
            terms = []
            for m in range(MODES):
                hb[rows8(at_row * MODES + m), :] = h[m]
                terms.append(rl[m * 8 : (m + 1) * 8, :] * h[m])
            while len(terms) > 1:
                terms = [terms[n] + terms[n + 1] for n in range(0, len(terms), 2)]
            ys[rows8(at_row), :] = terms[0]
        return h

    lax.fori_loop(
        0, ROWS // 2, forward,
        tuple(sin[pl.ds(m, TILES, stride=MODES), :] for m in range(MODES)),
    )
    gat_slot = ids(CHUNKS * (PLANE - 1))
    gat_in = []
    per = WIDE // 128
    for i in range(TILES):
        lanes = slice(128 * i, 128 * (i + 1))
        out = ys[pl.ds(i, ROWS, stride=8), :].astype(BF16)
        co[:, lanes] = out
        gated = (q_ref[:, lanes].astype(F32) * out.astype(F32)).astype(BF16)
        chunk, at_lane = i // per, i % per
        gat[chunk, mine, 128 * at_lane : 128 * (at_lane + 1)] = gated
        if at_lane == per - 1:
            gat_in.append([
                send(gat.at[chunk, mine], gat.at[chunk, mine], plane(k),
                     gat_slot + chunk * (PLANE - 1) + k - 1)
                for k in range(1, PLANE)
            ])

    mix(2, False)
    g_fwd.wait_recv()
    mix(3, False)
    for i in range(TILES):
        lanes = slice(128 * i, 128 * (i + 1))
        mixed = gm[:, lanes].astype(BF16).astype(F32)
        gq_ref[:, lanes] = (mixed * co[:, lanes].astype(F32)).astype(BF16)
        cot = (mixed * q_ref[:, lanes].astype(F32)).astype(BF16)
        cs[pl.ds(i, ROWS, stride=8), :] = cot.astype(F32)

    half = MODES // 2
    for part in range(2):
        modes = range(part * half, (part + 1) * half)

        def backward(n, carry, modes=modes):
            g, plain, ramp = carry
            for u in range(2):
                at_row = ROWS - 1 - (n * 2 + u)
                cot = cs[rows8(at_row), :]
                states = [hb[rows8(at_row * MODES + m), :] for m in modes]
                g = tuple(decay(m) * g[j] + cot for j, m in enumerate(modes))
                plain = tuple(plain[j] + states[j] * cot for j in range(half))
                ramp = tuple(ramp[j] + states[j] * g[j] for j in range(half))
            return g, plain, ramp

        found = lax.fori_loop(0, ROWS // 2, backward, ((zero,) * half,) * 3)
        for j, m in enumerate(modes):
            for n in range(3):
                ms[pl.ds(n * 16 + m, TILES, stride=64), :] = found[n][j]

    def reach(t, z):
        for u in range(2):
            z = tuple(
                decay(m) * (z[m] + hb[rows8((t * 2 + u) * MODES + m), :]) for m in range(MODES)
            )
        return z

    z = lax.fori_loop(0, ROWS // 2, reach, (zero,) * MODES)
    for m in range(MODES):
        ms[pl.ds(48 + m, TILES, stride=64), :] = z[m]
    slot = ids(PLANE - 1)
    m_in = [
        send(ms.at[tile((p + k) % PLANE, 64)], min.at[tile(p, 64)], plane(k), slot + k - 1)
        for k in range(1, PLANE)
    ]
    min[tile(p, 64), :] = ms[tile(p, 64), :]

    a_far.wait_recv()
    a_fwd = send(at.at[far], at.at[far], (s, sib), a_fwd_slot)
    a_sib.wait_recv()
    a_fwd.wait_recv()

    rs_slot = ids(CHUNKS * (LAYERS - 1))
    rs_in = []

    def product(chunk):
        for copy in gat_in[chunk]:
            copy.wait_recv()
        for k in range(1, LAYERS):
            there = (y + k) % LAYERS
            value = jnp.dot(at[there], gat[chunk], preferred_element_type=F32)
            rs_send[chunk, k - 1] = value.astype(BF16)
            rs_in.append(
                send(rs_send.at[chunk, k - 1], rs_recv.at[chunk, k - 1], layer(k),
                     rs_slot + chunk * (LAYERS - 1) + k - 1)
            )
        own[:, chunk * WIDE : (chunk + 1) * WIDE] = jnp.dot(
            at[y], gat[chunk], preferred_element_type=F32
        )

    product(0)

    for copy in m_in:
        copy.wait_recv()
    blank = jnp.zeros((MODES, 128), F32)
    state, plain, ramp, carried, power = blank, blank, blank, blank, blank + 1.0
    for b in reversed(range(PLANE)):
        g_b, p_b, q_b, z_b = (min[b * 64 + n * 16 : b * 64 + (n + 1) * 16, :] for n in range(4))
        to[b * 48 : b * 48 + 16, :] = state
        plain = plain + p_b
        ramp = ramp + q_b + state * z_b
        carried = carried + power * z_b
        state = step_w * state + g_b
        power = power * step_w
    here = y * 64
    for n, value in enumerate((state, plain, ramp, carried)):
        yin2[pl.ds(pl.multiple_of(here + n * 16, 16), 16), :] = value
    slot = ids(LAYERS - 1)
    y2_in = [
        send(yin2.at[tile(y, 64)], yin2.at[tile(y, 64)], layer(k), slot + k - 1)
        for k in range(1, LAYERS)
    ]

    product(1)

    for copy in y2_in:
        copy.wait_recv()
    after, chosen, plain, ramp = blank, blank, blank, blank
    for b in reversed(range(LAYERS)):
        g_b, p_b, q_b, z_b = (yin2[b * 64 + n * 16 : b * 64 + (n + 1) * 16, :] for n in range(4))
        plain = plain + p_b
        ramp = ramp + q_b + after * z_b
        chosen = jnp.where(b == y, after, chosen)
        after = layer_w * after + g_b
    root = jnp.sqrt(rate) * grad_scale
    grad_res = root * plain
    grad_log = res_ref[:, my_tile] * root * (0.5 * plain - rate * (ramp - plain))
    for b in reversed(range(PLANE)):
        to[b * 48 : b * 48 + 16, :] += chosen
        chosen = step_w * chosen
        to[b * 48 + 16 : b * 48 + 32, :] = grad_res
        to[b * 48 + 32 : b * 48 + 48, :] = grad_log
    slot = ids(PLANE - 1)
    t_in = [
        send(to.at[tile((p + k) % PLANE, 48)], tin.at[tile(p, 48)], plane(k), slot + k - 1)
        for k in range(1, PLANE)
    ]
    tin[tile(p, 48), :] = to[tile(p, 48), :]

    product(2)

    for copy in t_in:
        copy.wait_recv()
    for i in range(TILES):
        lanes = slice(128 * i, 128 * (i + 1))
        gr_ref[:, lanes] = tin[i * 48 + 16 : i * 48 + 32, :]
        gl_ref[:, lanes] = tin[i * 48 + 32 : i * 48 + 48, :]

    def final(n, g):
        for u in range(2):
            at_row = ROWS - 1 - (n * 2 + u)
            cot = cs[rows8(at_row), :]
            g = tuple(decay(m) * g[m] + cot for m in range(MODES))
            terms = [rl[m * 8 : (m + 1) * 8, :] * g[m] for m in range(MODES)]
            while len(terms) > 1:
                terms = [terms[n] + terms[n + 1] for n in range(0, len(terms), 2)]
            ys[rows8(at_row), :] = terms[0]
        return g

    lax.fori_loop(
        0, ROWS // 2, final,
        tuple(tin[pl.ds(m, TILES, stride=48), :] for m in range(MODES)),
    )
    for i in range(TILES):
        lanes = slice(128 * i, 128 * (i + 1))
        back = ys[pl.ds(i, ROWS, stride=8), :].astype(BF16).astype(F32)
        gk_ref[:, lanes] = (back * v_ref[:, lanes].astype(F32)).astype(BF16)
        gv_ref[:, lanes] = (back * k_ref[:, lanes].astype(F32)).astype(BF16)

    product(3)

    for copy in rs_in:
        copy.wait_recv()
    for chunk in range(CHUNKS):
        cols = slice(chunk * WIDE, (chunk + 1) * WIDE)
        total = own[:, cols]
        for k in range(LAYERS - 1):
            total = total + rs_recv[chunk, k].astype(F32)
        gw_ref[:, cols] = total * grad_scale
    for copy in sends:
        copy.wait_send()
    assert counter[0] <= SLOTS


SLOTS = 96


def per_device(query_act, key_act, value_act, residue, decay_rate, out_weight, grad_out):
    vmem = pl.BlockSpec(memory_space=pltpu.VMEM)
    shape = jax.ShapeDtypeStruct
    small = shape((ROWS, COLS), BF16)
    modal = shape((MODES, COLS), F32)
    scratch = [
        ((PARTS * DPART, COLS), BF16),
        ((ROWS * 8, 128), F32),
        ((ROWS * 8, 128), F32),
        ((ROWS * 8, 128), F32),
        ((ROWS * MODES * 8, 128), F32),
        ((MODES * 8, 128), F32),
        ((MODES * 8, 128), F32),
        ((PARTS, ROWS, DPART), BF16),
        ((PLANE, PIECE, ROWS), BF16),
        ((PARTS, PIECE, PLANE * ROWS), BF16),
        ((CHUNKS, PLANE * ROWS, WIDE), BF16),
        ((ROWS, COLS), F32),
        ((ROWS, COLS), BF16),
        ((TILES * 16, 128), F32),
        ((PLANE * 16, 128), F32),
        ((PLANE * 16, 128), F32),
        ((TILES * 16, 128), F32),
        ((LAYERS * 16, 128), F32),
        ((TILES * 64, 128), F32),
        ((PLANE * 64, 128), F32),
        ((LAYERS * 64, 128), F32),
        ((PLANE * 48, 128), F32),
        ((TILES * 48, 128), F32),
        ((CHUNKS, LAYERS - 1, PIECE, WIDE), BF16),
        ((CHUNKS, LAYERS - 1, PIECE, WIDE), BF16),
        ((PIECE, COLS), F32),
    ]
    return pl.pallas_call(
        body,
        out_shape=(small, small, small, shape((PIECE, COLS), F32), modal, modal),
        in_specs=[vmem] * 6 + [pl.BlockSpec(memory_space=pl.ANY)],
        out_specs=(vmem,) * 6,
        scratch_shapes=[pltpu.VMEM(*entry) for entry in scratch]
        + [
            pltpu.SemaphoreType.DMA((4,)),
            pltpu.SemaphoreType.DMA((SLOTS,)),
            pltpu.SemaphoreType.DMA((SLOTS,)),
        ],
        compiler_params=pltpu.CompilerParams(
            collective_id=0, has_side_effects=True, vmem_limit_bytes=56 * 2**20
        ),
        cost_estimate=pl.CostEstimate(
            flops=2 * 2**31, bytes_accessed=20 * 2**20, transcendentals=0
        ),
    )(query_act, key_act, value_act, grad_out, residue, decay_rate, out_weight)


def solution(mesh):
    both = P("seq", "chan")
    chan = P(None, "chan")
    return jax.shard_map(
        per_device,
        mesh=mesh,
        in_specs=(both, both, both, chan, chan, chan, both),
        out_specs=(both, both, both, both, chan, chan),
        check_vma=False,
    )
```

time: 897 us -> 105 us (0.12)
  waiting for transfers between devices: 539 us -> 0 us
  matrix products: 98.7 us -> 0 us
  Pallas kernels: 0 us -> 93.3 us
  local copies, waits for them, and re-layouts: 94.4 us -> 10.3 us
  blocking collectives: 72.4 us -> 0 us
  starting transfers between devices: 40.5 us -> 0 us
  other arithmetic: 28.5 us -> 0 us
  between operations: 14.5 us -> 0.64 us
    psum x1 -> x0, waiting for transfers between devices: 248 us -> none  [sequence_layout(): plain_sum, ramp_sum = lax.psum((plain_sum, ramp_sum), 'seq')]
    all_gather x2 -> x0, waiting for transfers between devices: 201 us -> none  [the longest x1 184 us: per_device(): lax.all_gather(gated_act, 'seq', axis=0, tiled=True)]
    dot_general x18 -> x0, matrix products: 98.7 us -> none  [the longest x16 84.2 us: apply_table(): return jnp.einsum('ft,atb->afb', matrix, values, precision=highest)]
    pallas_call x0 -> x1, Pallas kernels: none -> 93.3 us  [per_device(): pl.pallas_call(body, out_shape=(small, small, small, shape((PIECE, COLS),...]
    all_to_all x6 -> x0, waiting for transfers between devices: 89.5 us -> none  [the longest x1 30.5 us: sequence_layout(): lax.all_to_all(real_part.reshape(6, 1, tok_rows, chan_cols), 'seq', split...]
    all_to_all x2 -> x0, blocking collectives: 72.4 us -> none  [the longest x1 42.9 us: sequence_layout(): lax.all_to_all(real_part, 'seq', split_axis=1, concat_axis=2, tiled=True)]
    reshape x12 -> x0, local copies, waits for them, and re-layouts: 55.4 us -> none  [the longest x1 8.61 us: sequence_layout(): imag_part.reshape(6, 1, tok_rows, chan_cols)]
    all_to_all x6 -> x0, starting transfers between devices: 40.4 us -> none  [the longest x1 8.76 us: sequence_layout(): lax.all_to_all(conv_input[None], 'seq', split_axis=1, concat_axis=0, tile...]
  transfers between devices with their start and end apart: 9 -> 0, of which waited for: 8 -> 0; matrix products, arithmetic and copies ran while one was open for 9% -> 0% of each run, Pallas kernels for 0% -> 0%
where the time goes in v1:
time: 105 us; the launch traced here: 104 us
  Pallas kernels  93.3 us (89%)
  local copies, waits for them, and re-layouts  10.3 us (10%)
    pallas_call x1, Pallas kernels, per_device(): pl.pallas_call(body, out_shape=(small, small, small, shape((PIECE, COLS),...  93.3 us
    unnamed x6, local copies, waits for them, and re-layouts  10.3 us

profile of v1, /device:TPU:0, one launch (start us, length us, event | category | flops | bytes accessed | tf_op | source)
XLA Modules:
  0.0 104.2 jit_solution(17645854785051822195)
XLA Ops:
  0.6 93.3 %shard_map.118 = (bf16[128,1024]{1,0:T(8,128)(2,1)}, bf16[128,1024]{1,0:T(8,128)(2,1)}, bf16[128,1024]{1,0:T(8,128)(2,1)}, f32[256,1024]{1,0:T(8,128)}, f32[16,1024]{1,0:T(8,128)}, /*index=5*/f32[16,1024]{1,0:T(8,128)}) custom-call(bf16[128,1024]{1,0:T(8,128)(2,1)} %q_ref.1, bf16[128,1024]{1,0:T(8,128)(2,1)} %k_ref.1, bf16[128,1024]{1,0:T(8,128)(2,1)} %v_ref.1, ...), custom_call_target="tpu_custom_call" | custom-call | flops 4294967296 | bytes 20971520 | tf_op jit(solution)/shard_map/pallas_call | solution.py:425
  93.9 1.7 %copy.19 = bf16[128,1024]{1,0:T(8,128)(2,1)} copy(bf16[128,1024]{1,0:T(8,128)(2,1)} %get-tuple-element.12) | data formatting | bytes 524288
  95.6 1.7 %copy.20 = bf16[128,1024]{1,0:T(8,128)(2,1)} copy(bf16[128,1024]{1,0:T(8,128)(2,1)} %get-tuple-element.13) | data formatting | bytes 524288
  97.3 1.7 %copy.21 = bf16[128,1024]{1,0:T(8,128)(2,1)} copy(bf16[128,1024]{1,0:T(8,128)(2,1)} %get-tuple-element.14) | data formatting | bytes 524288
  98.9 2.3 %copy.22 = f32[256,1024]{1,0:T(8,128)} copy(f32[256,1024]{1,0:T(8,128)} %get-tuple-element.15) | data formatting | bytes 2097152
  101.2 1.5 %copy.23 = f32[16,1024]{1,0:T(8,128)} copy(f32[16,1024]{1,0:T(8,128)} %get-tuple-element.16) | data formatting | bytes 131072
  102.7 1.5 %copy.24 = f32[16,1024]{1,0:T(8,128)} copy(f32[16,1024]{1,0:T(8,128)} %get-tuple-element.17) | data formatting | bytes 131072

commit v2 on v1

--- a/solution.py
+++ b/solution.py
@@ -29,7 +29,7 @@
 def body(
     q_ref, k_ref, v_ref, g_ref, res_ref, rate_ref, w_ref,
     gq_ref, gk_ref, gv_ref, gw_ref, gr_ref, gl_ref,
-    wv, xs, cs, ys, hb, al, rl, gall, gt, at, gat, gm, co,
+    wv, xs, cs, ys, hb, al, rl, gall, gt, turned, at, gat, gm, co,
     hs, hin, so, sin, yin, ms, min, yin2, to, tin,
     rs_send, rs_recv, own, wsem, ssem, rsem,
 ):
@@ -47,6 +47,12 @@
     def plane(k):
         return (y * PLANE + (p + k) % PLANE, c)
 
+    def across(k):
+        return (y * PLANE + (p + 2 * k) % PLANE, c)
+
+    def place(x_step, z_turn):
+        return ((p // 2 + x_step) % 4) * 2 + (p % 2 + z_turn) % 2
+
     def layer(k):
         return (((y + k) % LAYERS) * PLANE + p, c)
 
@@ -74,6 +80,7 @@
     barrier = pltpu.get_barrier_semaphore()
     greeted = [plane(k) for k in range(1, PLANE)] + [layer(k) for k in range(1, LAYERS)]
     greeted += [(s, sib), (s, far)]
+    greeted += [(y * PLANE + place(k, 1), far) for k in range(4)]
     for device in greeted:
         pl.semaphore_signal(barrier, inc=1, device_id=device, device_id_type=MESH)
 
@@ -110,20 +117,31 @@
         send(hs.at[tile((p + k) % PLANE, 16)], hin.at[tile(p, 16)], plane(k), slot + k - 1)
         for k in range(1, PLANE)
     ]
-    slot = ids(3)
-    g_far = send(g_ref, gall.at[c], (s, far), slot)
-    g_sib = send(g_ref, gall.at[c], (s, sib), slot + 1)
-    g_fwd_slot = slot + 2
+    slot = ids(9)
+    g_sib = send(g_ref, gall.at[c], (s, sib), slot)
+
+    g_slot = slot
+
+    def far_part(j):
+        cols = pl.ds(j * DEPTH, DEPTH)
+        return send(g_ref.at[:, cols], gall.at[c, :, cols], (s, far), g_slot + 1 + j)
+
+    def far_pass(j):
+        cols = pl.ds(j * DEPTH, DEPTH)
+        g_far[j].wait_recv()
+        return send(gall.at[far, :, cols], gall.at[far, :, cols], (s, sib), g_slot + 5 + j)
+
+    g_far = [far_part(0), far_part(1)]
     hin[tile(p, 16), :] = hs[tile(p, 16), :]
     gall[c] = g_ref[...]
 
     for k in range(PLANE):
         gt[k] = g_ref[:, PIECE * k : PIECE * (k + 1)].T
-    slot = ids(PLANE - 1)
+    slot = ids(11)
+    a_slot = slot
     mine = pl.ds(pl.multiple_of(p * ROWS, ROWS), ROWS)
-    a_in = [
-        send(gt.at[(p + k) % PLANE], at.at[c, :, mine], plane(k), slot + k - 1)
-        for k in range(1, PLANE)
+    a_near = [
+        send(gt.at[place(k, 0)], at.at[c, :, mine], across(k), slot + k - 1) for k in range(1, 4)
     ]
     at[c, :, mine] = gt[p]
 
@@ -175,14 +193,8 @@
     ]
     sin[tile(p, 16), :] = so[tile(p, 16), :]
 
-    for copy in a_in:
-        copy.wait_recv()
-    slot = ids(3)
-    a_far = send(at.at[c], at.at[c], (s, far), slot)
-    a_sib = send(at.at[c], at.at[c], (s, sib), slot + 1)
-    a_fwd_slot = slot + 2
-    g_far.wait_recv()
-    g_fwd = send(gall.at[far], gall.at[far], (s, sib), g_fwd_slot)
+    g_far += [far_part(2), far_part(3)]
+    g_pass = [far_pass(0), far_pass(1)]
 
     for copy in s_in:
         copy.wait_recv()
@@ -205,8 +217,6 @@
         0, ROWS // 2, forward,
         tuple(sin[pl.ds(m, TILES, stride=MODES), :] for m in range(MODES)),
     )
-    gat_slot = ids(CHUNKS * (PLANE - 1))
-    gat_in = []
     per = WIDE // 128
     for i in range(TILES):
         lanes = slice(128 * i, 128 * (i + 1))
@@ -215,15 +225,40 @@
         gated = (q_ref[:, lanes].astype(F32) * out.astype(F32)).astype(BF16)
         chunk, at_lane = i // per, i % per
         gat[chunk, mine, 128 * at_lane : 128 * (at_lane + 1)] = gated
-        if at_lane == per - 1:
-            gat_in.append([
-                send(gat.at[chunk, mine], gat.at[chunk, mine], plane(k),
-                     gat_slot + chunk * (PLANE - 1) + k - 1)
-                for k in range(1, PLANE)
-            ])
-
+
+    gat_slot = ids(CHUNKS * (PLANE - 1))
+    other = place(0, 1)
+    theirs = pl.ds(pl.multiple_of(other * ROWS, ROWS), ROWS)
+    gat_z, gat_in = [], []
+
+    def spread(chunk):
+        slot = gat_slot + chunk * (PLANE - 1)
+        block = gat.at[chunk, mine]
+        gat_z.append(send(block, block, (y * PLANE + other, c), slot))
+        gat_in.append([send(block, block, across(k), slot + k) for k in (1, 3, 2)])
+
+    def spread_more(chunk):
+        slot = gat_slot + chunk * (PLANE - 1) + 3
+        block = gat.at[chunk, theirs]
+        gat_z[chunk].wait_recv()
+        gat_in[chunk] += [send(block, block, across(k), slot + k) for k in (1, 3, 2)]
+
+    spread(0)
+
+    a_near += [
+        send(gt.at[place(k, 1)], at.at[c, :, mine], (y * PLANE + place(k, 1), c), a_slot + 3 + k)
+        for k in range(4)
+    ]
+    a_cross = [
+        send(gt.at[place(k, 1)], at.at[c, :, mine], (y * PLANE + place(k, 1), far), a_slot + 7 + k)
+        for k in range(4)
+    ]
+
+    g_pass += [far_pass(2), far_pass(3)]
     mix(2, False)
-    g_fwd.wait_recv()
+    spread_more(0)
+    for copy in g_pass:
+        copy.wait_recv()
     mix(3, False)
     for i in range(TILES):
         lanes = slice(128 * i, 128 * (i + 1))
@@ -269,10 +304,21 @@
     ]
     min[tile(p, 64), :] = ms[tile(p, 64), :]
 
-    a_far.wait_recv()
-    a_fwd = send(at.at[far], at.at[far], (s, sib), a_fwd_slot)
-    a_sib.wait_recv()
-    a_fwd.wait_recv()
+    slot = ids(5)
+    for k in range(4):
+        turned[k] = gall[far, :, pl.ds(pl.multiple_of(place(k, 0) * PIECE, PIECE), PIECE)].T
+    a_cross += [
+        send(turned.at[k], at.at[far, :, mine], across(k), slot + k - 1) for k in range(1, 4)
+    ]
+    at[far, :, mine] = turned[0]
+    spread(1)
+    for copy in a_near:
+        copy.wait_recv()
+    a_sib = [send(at.at[c], at.at[c], (s, sib), slot + 3)]
+    for copy in a_cross:
+        copy.wait_recv()
+    a_sib.append(send(at.at[far], at.at[far], (s, sib), slot + 4))
+    spread_more(1)
 
     rs_slot = ids(CHUNKS * (LAYERS - 1))
     rs_in = []
@@ -291,8 +337,6 @@
         own[:, chunk * WIDE : (chunk + 1) * WIDE] = jnp.dot(
             at[y], gat[chunk], preferred_element_type=F32
         )
-
-    product(0)
 
     for copy in m_in:
         copy.wait_recv()
@@ -315,7 +359,10 @@
         for k in range(1, LAYERS)
     ]
 
-    product(1)
+    for copy in a_sib:
+        copy.wait_recv()
+    product(0)
+    spread(2)
 
     for copy in y2_in:
         copy.wait_recv()
@@ -341,7 +388,9 @@
     ]
     tin[tile(p, 48), :] = to[tile(p, 48), :]
 
-    product(2)
+    product(1)
+    spread_more(2)
+    spread(3)
 
     for copy in t_in:
         copy.wait_recv()
@@ -371,6 +420,8 @@
         gk_ref[:, lanes] = (back * v_ref[:, lanes].astype(F32)).astype(BF16)
         gv_ref[:, lanes] = (back * k_ref[:, lanes].astype(F32)).astype(BF16)
 
+    spread_more(3)
+    product(2)
     product(3)
 
     for copy in rs_in:
@@ -386,7 +437,13 @@
     assert counter[0] <= SLOTS
 
 
-SLOTS = 96
+SLOTS = 112
+
+
+def settle(*refs):
+    count = len(refs) // 2
+    for n in range(count):
+        refs[count + n][...] = refs[n][...]
 
 
 def per_device(query_act, key_act, value_act, residue, decay_rate, out_weight, grad_out):
@@ -404,6 +461,7 @@
         ((MODES * 8, 128), F32),
         ((PARTS, ROWS, DPART), BF16),
         ((PLANE, PIECE, ROWS), BF16),
+        ((4, PIECE, ROWS), BF16),
         ((PARTS, PIECE, PLANE * ROWS), BF16),
         ((CHUNKS, PLANE * ROWS, WIDE), BF16),
         ((ROWS, COLS), F32),
@@ -422,9 +480,10 @@
         ((CHUNKS, LAYERS - 1, PIECE, WIDE), BF16),
         ((PIECE, COLS), F32),
     ]
-    return pl.pallas_call(
+    outs = (small, small, small, shape((PIECE, COLS), F32), modal, modal)
+    found = pl.pallas_call(
         body,
-        out_shape=(small, small, small, shape((PIECE, COLS), F32), modal, modal),
+        out_shape=outs,
         in_specs=[vmem] * 6 + [pl.BlockSpec(memory_space=pl.ANY)],
         out_specs=(vmem,) * 6,
         scratch_shapes=[pltpu.VMEM(*entry) for entry in scratch]
@@ -440,6 +499,12 @@
             flops=2 * 2**31, bytes_accessed=20 * 2**20, transcendentals=0
         ),
     )(query_act, key_act, value_act, grad_out, residue, decay_rate, out_weight)
+    return pl.pallas_call(
+        settle,
+        out_shape=outs,
+        in_specs=[vmem] * len(outs),
+        out_specs=(vmem,) * len(outs),
+    )(*found)
 
 
 def solution(mesh):

time: 105 us -> 78.8 us (0.75)
  Pallas kernels: 93.3 us -> 77.3 us
  local copies, waits for them, and re-layouts: 10.3 us -> 0 us
    pallas_call x1 -> x2, Pallas kernels: 93.3 us -> 77.3 us  [the longest x1 74.6 us: per_device(): pl.pallas_call(body, out_shape=outs, in_specs=[vmem] * 6 + [pl.BlockSpec(...]
    unnamed x6 -> x0, local copies, waits for them, and re-layouts: 10.3 us -> none
where the time goes in v2:
time: 78.8 us; the launch traced here: 78 us
  Pallas kernels  77.3 us (98%)
    pallas_call x1, Pallas kernels, per_device(): pl.pallas_call(body, out_shape=outs, in_specs=[vmem] * 6 + [pl.BlockSpec(...  74.6 us
    pallas_call x1, Pallas kernels, per_device(): pl.pallas_call(settle, out_shape=outs, in_specs=[vmem] * len(outs), out_s...  2.71 us

profile of v2, /device:TPU:0, one launch (start us, length us, event | category | flops | bytes accessed | tf_op | source)
XLA Modules:
  0.0 78.0 jit_solution(3908680115882594202)
XLA Ops:
  0.6 74.6 %shard_map.118 = (bf16[128,1024]{1,0:T(8,128)(2,1)}, bf16[128,1024]{1,0:T(8,128)(2,1)}, bf16[128,1024]{1,0:T(8,128)(2,1)}, f32[256,1024]{1,0:T(8,128)}, f32[16,1024]{1,0:T(8,128)}, /*index=5*/f32[16,1024]{1,0:T(8,128)}) custom-call(bf16[128,1024]{1,0:T(8,128)(2,1)} %q_ref.1, bf16[128,1024]{1,0:T(8,128)(2,1)} %k_ref.1, bf16[128,1024]{1,0:T(8,128)(2,1)} %v_ref.1, ...), custom_call_target="tpu_custom_call" | custom-call | flops 4294967296 | bytes 20971520 | tf_op jit(solution)/shard_map/pallas_call | solution.py:484
  75.3 2.7 %shard_map.119 = (bf16[128,1024]{1,0:T(8,128)(2,1)}, bf16[128,1024]{1,0:T(8,128)(2,1)}, bf16[128,1024]{1,0:T(8,128)(2,1)}, f32[256,1024]{1,0:T(8,128)}, f32[16,1024]{1,0:T(8,128)}, /*index=5*/f32[16,1024]{1,0:T(8,128)}) custom-call(bf16[128,1024]{1,0:T(8,128)(2,1)} %get-tuple-element.12.refs_0_, bf16[128,1024]{1,0:T(8,128)(2,1)} %get-tuple-element.13.refs_1_, ...), custom_call_target="tpu_custom_call" | custom-call | tf_op jit(solution)/shard_map/pallas_call | solution.py:502

commit v3 on v1

v3 whole, which is shorter than its diff:
```python
import jax
import jax.numpy as jnp
from jax import lax
from jax.experimental import pallas as pl
from jax.experimental.pallas import tpu as pltpu
from jax.sharding import PartitionSpec as P

MESH = pl.DeviceIdType.MESH
F32 = jnp.float32
BF16 = jnp.bfloat16
ROWS = 128
COLS = 1024
TILES = 8
MODES = 16
PLANE = 8
LAYERS = 4
PARTS = 4
DPART = 2048
PIECE = 256
WIDTHS = (256, 256, 256, 128, 128)
CHUNKS = len(WIDTHS)
RELAYED = 3
DEPTH = 512


def rows8(index):
    return pl.ds(pl.multiple_of(index * 8, 8), 8)


def body(
    q_hbm, k_hbm, v_hbm, g_hbm, res_hbm, rate_hbm, w_ref,
    gq_ref, gk_ref, gv_ref, gw_ref, gr_ref, gl_ref,
    q_ref, k_ref, v_ref, g_ref, res_ref, rate_ref,
    wv, xs, cs, ys, hb, al, rl, gall, gt, turned, at, gat, gm, co,
    hs, hin, so, sin, yin, gs, gin, yin2, to, tin, pq, pin, yp, pr, prin,
    rs_send, rs_recv, relay_send, relay_recv, held, own, wsem, ssem, rsem,
):
    s = lax.axis_index("seq")
    c = lax.axis_index("chan")
    y = s // PLANE
    p = s % PLANE
    sib = (c // 2) * 2 + (1 - c % 2)
    far = (c + 2) % PARTS
    farsib = (sib + 2) % PARTS
    grad_scale = float(ROWS * PLANE * LAYERS) ** -0.5
    counter = [0]
    sends = []

    def plane(k):
        return (y * PLANE + (p + k) % PLANE, c)

    def across(k):
        return (y * PLANE + (p + 2 * k) % PLANE, c)

    def place(x_step, z_turn):
        return ((p // 2 + x_step) % 4) * 2 + (p % 2 + z_turn) % 2

    def layer(k):
        return (((y + k) % LAYERS) * PLANE + p, c)

    def ids(count):
        counter[0] += count
        assert counter[0] <= SLOTS
        return counter[0] - count

    def send(src, dst, device, slot):
        copy = pltpu.make_async_remote_copy(
            src_ref=src, dst_ref=dst, send_sem=ssem.at[slot], recv_sem=rsem.at[slot],
            device_id=device, device_id_type=MESH,
        )
        copy.start()
        sends.append(copy)
        return copy

    def tile(index, size):
        return pl.ds(pl.multiple_of(index * size, size), size)

    def decay(m):
        return al[m * 8 : (m + 1) * 8, :]

    def amplitude(m):
        return rl[m * 8 : (m + 1) * 8, :]

    def tree(terms):
        while len(terms) > 1:
            terms = [terms[n] + terms[n + 1] for n in range(0, len(terms), 2)]
        return terms[0]

    barrier = pltpu.get_barrier_semaphore()
    greeted = [plane(k) for k in range(1, PLANE)] + [layer(k) for k in range(1, LAYERS)]
    greeted += [(s, sib), (s, far)]
    greeted += [(y * PLANE + place(k, 1), far) for k in range(4)]
    for device in greeted:
        pl.semaphore_signal(barrier, inc=1, device_id=device, device_id_type=MESH)

    loads = {}
    for n, (name, src, dst) in enumerate((
        ("rate", rate_hbm, rate_ref), ("k", k_hbm, k_ref), ("v", v_hbm, v_ref),
        ("res", res_hbm, res_ref), ("g", g_hbm, g_ref), ("q", q_hbm, q_ref),
    )):
        loads[name] = pltpu.make_async_copy(src, dst, wsem.at[PARTS + n])
        loads[name].start()
    order = (c, sib, far, farsib)
    wcopies = []
    for n, h in enumerate(order):
        part = tile(h, DPART)
        copy = pltpu.make_async_copy(w_ref.at[part], wv.at[part], wsem.at[n])
        copy.start()
        wcopies.append(copy)

    for name in ("rate", "k", "v"):
        loads[name].wait()
    for i in range(TILES):
        lanes = slice(128 * i, 128 * (i + 1))
        al[pl.ds(i, MODES, stride=8), :] = jnp.exp(-rate_ref[:, lanes])
        x = (k_ref[:, lanes].astype(F32) * v_ref[:, lanes].astype(F32)).astype(BF16)
        xs[pl.ds(i, ROWS, stride=8), :] = x.astype(F32)

    zero = jnp.zeros((8, 128), F32)

    def ahead(t, h):
        for u in range(4):
            x = xs[rows8(t * 4 + u), :]
            h = tuple(decay(m) * h[m] + x for m in range(MODES))
        return h

    h = lax.fori_loop(0, ROWS // 4, ahead, (zero,) * MODES)
    for m in range(MODES):
        hs[pl.ds(m, TILES, stride=MODES), :] = h[m]

    pl.semaphore_wait(barrier, len(greeted))

    def to_owners(src, dst, size):
        slot = ids(PLANE - 1)
        copies = [
            send(src.at[tile((p + k) % PLANE, size)], dst.at[tile(p, size)], plane(k), slot + k - 1)
            for k in range(1, PLANE)
        ]
        dst[tile(p, size), :] = src[tile(p, size), :]
        return copies

    def to_layers(ref, size):
        slot = ids(LAYERS - 1)
        block = ref.at[tile(y, size)]
        return [send(block, block, layer(k), slot + k - 1) for k in range(1, LAYERS)]

    def arrive(copies):
        for copy in copies:
            copy.wait_recv()

    h_in = to_owners(hs, hin, 16)
    loads["g"].wait()
    g_slot = ids(9)
    g_sib = send(g_ref, gall.at[c], (s, sib), g_slot)

    def far_cols(n):
        return tile((p // 2 + n) % 4, DEPTH)

    def far_part(n):
        cols = far_cols(n)
        g_far[n] = send(g_ref.at[:, cols], gall.at[c, :, cols], (s, far), g_slot + 1 + n)

    def far_pass(n):
        cols = far_cols(n)
        g_far[n].wait_recv()
        block = gall.at[far, :, cols]
        g_pass[n] = send(block, block, (s, sib), g_slot + 5 + n)
        turned[n] = gall[far, :, tile(place(n, 0), PIECE)].T
        if n == 0:
            at[far, :, mine] = turned[0]
        else:
            a_cross.append(
                send(turned.at[n], at.at[far, :, mine], across(n), a_slot + 10 + n)
            )
        mix(2, n)

    g_far, g_pass = {}, {}
    gall[c] = g_ref[...]

    for k in range(PLANE):
        gt[k] = g_ref[:, PIECE * k : PIECE * (k + 1)].T
    a_slot = ids(16)
    mine = tile(p, ROWS)
    a_near = [
        send(gt.at[place(k, 0)], at.at[c, :, mine], across(k), a_slot + k - 1) for k in range(1, 4)
    ]
    at[c, :, mine] = gt[p]
    a_near += [
        send(gt.at[place(k, 1)], at.at[c, :, mine], (y * PLANE + place(k, 1), c), a_slot + 3 + k)
        for k in range(4)
    ]
    a_cross = [
        send(gt.at[place(k, 1)], at.at[c, :, mine], (y * PLANE + place(k, 1), far), a_slot + 7 + k)
        for k in range(4)
    ]
    far_part(1)

    seen = set()

    def mix(n, j):
        h = order[n]
        if n not in seen:
            seen.add(n)
            wcopies[n].wait()
        if n >= 2:
            j = (p // 2 + j) % 4
        deep = pl.ds(pl.multiple_of(h * DPART + j * DEPTH, DEPTH), DEPTH)
        cols = tile(j, DEPTH)
        gm[...] += jnp.dot(gall[h, :, cols], wv[deep, :], preferred_element_type=F32)

    gm[...] = jnp.zeros_like(gm)
    loads["res"].wait()
    for i in range(TILES):
        lanes = slice(128 * i, 128 * (i + 1))
        rl[pl.ds(i, MODES, stride=8), :] = res_ref[:, lanes] * jnp.sqrt(rate_ref[:, lanes])
    for j in range(4):
        mix(0, j)

    rate = rate_ref[:, tile(p, 128)]
    step_w = jnp.exp(-float(ROWS) * rate)
    layer_w = jnp.exp(-float(ROWS * PLANE) * rate)
    blank = jnp.zeros((MODES, 128), F32)
    arrive(h_in)
    state = blank
    for b in range(PLANE):
        so[b * 16 : (b + 1) * 16, :] = state
        state = step_w * state + hin[b * 16 : (b + 1) * 16, :]
    yin[tile(y, 16), :] = state
    y_in = to_layers(yin, 16)
    g_sib.wait_recv()
    for j in range(4):
        mix(1, j)
    arrive(y_in)
    before = blank
    for b in range(LAYERS):
        before = jnp.where(b < y, layer_w * before + yin[b * 16 : (b + 1) * 16, :], before)
    for b in range(PLANE):
        so[b * 16 : (b + 1) * 16, :] += before
        before = step_w * before
    s_in = to_owners(so, sin, 16)
    far_part(2)
    far_part(3)
    far_pass(1)

    loads["q"].wait()
    arrive(s_in)

    def forward(t, h):
        for u in range(2):
            at_row = t * 2 + u
            x = xs[rows8(at_row), :]
            h = tuple(decay(m) * h[m] + x for m in range(MODES))
            for m in range(MODES):
                hb[rows8(at_row * MODES + m), :] = h[m]
            ys[rows8(at_row), :] = tree([amplitude(m) * h[m] for m in range(MODES)])
        return h

    lax.fori_loop(
        0, ROWS // 2, forward,
        tuple(sin[pl.ds(m, TILES, stride=MODES), :] for m in range(MODES)),
    )

    gat_slot = ids(CHUNKS * (PLANE - 1))
    other = place(0, 1)
    theirs = tile(other, ROWS)
    distant = tile(place(2, 0), ROWS)
    gat_z, gat_x2, gat_in = [], [], []

    def spread(chunk):
        slot = gat_slot + chunk * (PLANE - 1)
        block = gat[chunk].at[mine]
        gat_z.append(send(block, block, (y * PLANE + other, c), slot))
        gat_x2.append(send(block, block, across(2), slot + 2))
        gat_in.append([send(block, block, across(k), slot + k) for k in (1, 3)])

    def spread_more(chunk):
        slot = gat_slot + chunk * (PLANE - 1) + 4
        block = gat[chunk].at[theirs]
        gat_z[chunk].wait_recv()
        gat_in[chunk] += [send(block, block, across(k), slot + k // 2) for k in (1, 3)]
        if chunk in straight:
            gat_in[chunk] += [gat_x2[chunk], send(block, block, across(2), slot + 2)]
            return
        block = gat[chunk].at[distant]
        gat_x2[chunk].wait_recv()
        gat_in[chunk].append(send(block, block, (y * PLANE + other, c), slot + 2))

    straight = (0,)
    starts = [sum(WIDTHS[:n]) for n in range(CHUNKS)]
    for i in range(TILES):
        lanes = slice(128 * i, 128 * (i + 1))
        out = ys[pl.ds(i, ROWS, stride=8), :].astype(BF16)
        co[:, lanes] = out
        gated = (q_ref[:, lanes].astype(F32) * out.astype(F32)).astype(BF16)
        chunk = max(n for n in range(CHUNKS) if starts[n] <= 128 * i)
        from_lane = 128 * i - starts[chunk]
        gat[chunk][mine, from_lane : from_lane + 128] = gated
        if 128 * (i + 1) == WIDTHS[0]:
            spread(0)

    far_part(0)
    far_pass(2)
    g_pass[1].wait_recv()
    mix(3, 1)
    far_pass(3)
    spread(1)
    g_pass[2].wait_recv()
    mix(3, 2)
    arrive(a_near)
    a_sib = [send(at.at[c], at.at[c], (s, sib), a_slot + 14)]
    spread_more(0)
    g_pass[3].wait_recv()
    mix(3, 3)
    far_pass(0)
    arrive(a_cross)
    a_sib.append(send(at.at[far], at.at[far], (s, sib), a_slot + 15))
    g_pass[0].wait_recv()
    mix(3, 0)
    for i in range(TILES):
        lanes = slice(128 * i, 128 * (i + 1))
        mixed = gm[:, lanes].astype(BF16).astype(F32)
        gq_ref[:, lanes] = (mixed * co[:, lanes].astype(F32)).astype(BF16)
        cot = (mixed * q_ref[:, lanes].astype(F32)).astype(BF16)
        cs[pl.ds(i, ROWS, stride=8), :] = cot.astype(F32)

    def behind(n, g):
        for u in range(4):
            cot = cs[rows8(ROWS - 1 - (n * 4 + u)), :]
            g = tuple(decay(m) * g[m] + cot for m in range(MODES))
        return g

    g = lax.fori_loop(0, ROWS // 4, behind, (zero,) * MODES)
    for m in range(MODES):
        gs[pl.ds(m, TILES, stride=MODES), :] = g[m]
    g_in = to_owners(gs, gin, 16)
    spread(2)
    spread_more(1)
    spread(3)

    half = MODES // 2
    for part in range(2):
        modes = range(part * half, (part + 1) * half)

        def backward(n, carry, modes=modes):
            g, plain, ramp = carry
            for u in range(2):
                at_row = ROWS - 1 - (n * 2 + u)
                cot = cs[rows8(at_row), :]
                states = [hb[rows8(at_row * MODES + m), :] for m in modes]
                g = tuple(decay(m) * g[j] + cot for j, m in enumerate(modes))
                plain = tuple(plain[j] + states[j] * cot for j in range(half))
                ramp = tuple(ramp[j] + states[j] * g[j] for j in range(half))
            return g, plain, ramp

        found = lax.fori_loop(0, ROWS // 2, backward, ((zero,) * half,) * 3)
        for j, m in enumerate(modes):
            for n in range(2):
                pq[pl.ds(n * 16 + m, TILES, stride=48), :] = found[n + 1][j]

    rs_slot = ids(CHUNKS * 3)
    relay_slot = ids(RELAYED * 2)
    rs_in, relay_in = [], []
    top, low = pl.ds(0, PIECE // 2), pl.ds(PIECE // 2, PIECE // 2)

    def partial(chunk, k):
        return jnp.dot(at[(y + k) % LAYERS], gat[chunk][...], preferred_element_type=F32)

    def product(chunk):
        arrive(gat_in[chunk])
        slot = rs_slot + chunk * 3
        value = partial(chunk, 2).astype(BF16)
        if chunk < RELAYED:
            relay_send[chunk][...] = value
            relay_in.append([
                send(relay_send[chunk].at[rows], relay_recv[chunk].at[rows], layer(k),
                     relay_slot + chunk * 2 + n)
                for n, (rows, k) in enumerate(((top, 1), (low, 3)))
            ])
            for n, k in enumerate((1, 3)):
                held[chunk][n] = partial(chunk, k)
        else:
            for n, k in ((2, 2), (0, 1), (1, 3)):
                rs_send[chunk][n] = value if k == 2 else partial(chunk, k).astype(BF16)
                rs_in.append(
                    send(rs_send[chunk].at[n], rs_recv[chunk].at[n], layer(k), slot + n)
                )
        own[:, starts[chunk] : starts[chunk] + WIDTHS[chunk]] = partial(chunk, 0)

    def pass_on(chunk):
        arrive(relay_in[chunk])
        for n, (k, added, alone) in enumerate(((1, top, low), (3, low, top))):
            value = held[chunk][n, added, :] + relay_recv[chunk][added, :].astype(F32)
            rs_send[chunk][n, added, :] = value.astype(BF16)
            rs_send[chunk][n, alone, :] = held[chunk][n, alone, :].astype(BF16)
            rs_in.append(
                send(rs_send[chunk].at[n], rs_recv[chunk].at[n], layer(k), rs_slot + chunk * 3 + n)
            )

    arrive(a_sib)
    product(0)
    spread_more(2)
    spread(4)

    arrive(g_in)
    state = blank
    for b in reversed(range(PLANE)):
        to[b * 16 : b * 16 + 16, :] = state
        state = step_w * state + gin[b * 16 : b * 16 + 16, :]
    yin2[tile(y, 16), :] = state
    y2_in = to_layers(yin2, 16)

    def reach(t, z):
        for u in range(2):
            z = tuple(
                decay(m) * (z[m] + hb[rows8((t * 2 + u) * MODES + m), :]) for m in range(MODES)
            )
        return z

    z = lax.fori_loop(0, ROWS // 2, reach, (zero,) * MODES)
    for m in range(MODES):
        pq[pl.ds(32 + m, TILES, stride=48), :] = z[m]

    pass_on(0)
    product(1)
    spread_more(3)

    arrive(y2_in)
    after, chosen = blank, blank
    for b in reversed(range(LAYERS)):
        chosen = jnp.where(b == y, after, chosen)
        after = layer_w * after + yin2[b * 16 : b * 16 + 16, :]
    for b in reversed(range(PLANE)):
        to[b * 16 : b * 16 + 16, :] += chosen
        chosen = step_w * chosen
    t_in = to_owners(to, tin, 16)
    p_in = to_owners(pq, pin, 48)
    pass_on(1)
    product(2)
    spread_more(4)

    arrive(p_in)
    plain, ramp = blank, blank
    for b in range(PLANE):
        p_b, q_b, z_b = (pin[b * 48 + n * 16 : b * 48 + (n + 1) * 16, :] for n in range(3))
        plain = plain + p_b
        ramp = ramp + q_b + to[b * 16 : b * 16 + 16, :] * z_b
    yp[pl.ds(pl.multiple_of(y * 32, 16), 16), :] = plain
    yp[pl.ds(pl.multiple_of(y * 32 + 16, 16), 16), :] = ramp
    yp_in = to_layers(yp, 32)

    arrive(t_in)

    def final(n, g):
        for u in range(2):
            at_row = ROWS - 1 - (n * 2 + u)
            cot = cs[rows8(at_row), :]
            g = tuple(decay(m) * g[m] + cot for m in range(MODES))
            ys[rows8(at_row), :] = tree([amplitude(m) * g[m] for m in range(MODES)])
        return g

    lax.fori_loop(
        0, ROWS // 2, final,
        tuple(tin[pl.ds(m, TILES, stride=MODES), :] for m in range(MODES)),
    )
    for i in range(TILES):
        lanes = slice(128 * i, 128 * (i + 1))
        back = ys[pl.ds(i, ROWS, stride=8), :].astype(BF16).astype(F32)
        gk_ref[:, lanes] = (back * v_ref[:, lanes].astype(F32)).astype(BF16)
        gv_ref[:, lanes] = (back * k_ref[:, lanes].astype(F32)).astype(BF16)

    pass_on(2)
    product(3)
    product(4)

    arrive(yp_in)
    plain, ramp = blank, blank
    for b in range(LAYERS):
        plain = plain + yp[b * 32 : b * 32 + 16, :]
        ramp = ramp + yp[b * 32 + 16 : b * 32 + 32, :]
    root = jnp.sqrt(rate) * grad_scale
    pr[0:16, :] = root * plain
    pr[16:32, :] = res_ref[:, tile(p, 128)] * root * (0.5 * plain - rate * (ramp - plain))
    slot = ids(PLANE - 1)
    pr_in = [send(pr, prin.at[tile(p, 32)], plane(k), slot + k - 1) for k in range(1, PLANE)]
    prin[tile(p, 32), :] = pr[...]

    arrive(pr_in)
    for i in range(TILES):
        lanes = slice(128 * i, 128 * (i + 1))
        gr_ref[:, lanes] = prin[i * 32 : i * 32 + 16, :]
        gl_ref[:, lanes] = prin[i * 32 + 16 : i * 32 + 32, :]
    arrive(rs_in)
    for chunk in range(CHUNKS):
        cols = slice(starts[chunk], starts[chunk] + WIDTHS[chunk])
        total = own[:, cols]
        for k in range(2 if chunk < RELAYED else 3):
            total = total + rs_recv[chunk][k].astype(F32)
        gw_ref[:, cols] = total * grad_scale
    for copy in sends:
        copy.wait_send()


SLOTS = 160


def settle(*refs):
    count = len(refs) // 2
    for n in range(count):
        refs[count + n][...] = refs[n][...]


def per_device(query_act, key_act, value_act, residue, decay_rate, out_weight, grad_out):
    vmem = pl.BlockSpec(memory_space=pltpu.VMEM)
    shape = jax.ShapeDtypeStruct
    small = shape((ROWS, COLS), BF16)
    modal = shape((MODES, COLS), F32)
    scratch = [
        ((ROWS, COLS), BF16),
        ((ROWS, COLS), BF16),
        ((ROWS, COLS), BF16),
        ((ROWS, DPART), BF16),
        ((MODES, COLS), F32),
        ((MODES, COLS), F32),
        ((PARTS * DPART, COLS), BF16),
        ((ROWS * 8, 128), F32),
        ((ROWS * 8, 128), F32),
        ((ROWS * 8, 128), F32),
        ((ROWS * MODES * 8, 128), F32),
        ((MODES * 8, 128), F32),
        ((MODES * 8, 128), F32),
        ((PARTS, ROWS, DPART), BF16),
        ((PLANE, PIECE, ROWS), BF16),
        ((4, PIECE, ROWS), BF16),
        ((PARTS, PIECE, PLANE * ROWS), BF16),
        [((PLANE * ROWS, wide), BF16) for wide in WIDTHS],
        ((ROWS, COLS), F32),
        ((ROWS, COLS), BF16),
        ((TILES * 16, 128), F32),
        ((PLANE * 16, 128), F32),
        ((PLANE * 16, 128), F32),
        ((TILES * 16, 128), F32),
        ((LAYERS * 16, 128), F32),
        ((TILES * 16, 128), F32),
        ((PLANE * 16, 128), F32),
        ((LAYERS * 16, 128), F32),
        ((PLANE * 16, 128), F32),
        ((TILES * 16, 128), F32),
        ((TILES * 48, 128), F32),
        ((PLANE * 48, 128), F32),
        ((LAYERS * 32, 128), F32),
        ((32, 128), F32),
        ((TILES * 32, 128), F32),
        [((3, PIECE, wide), BF16) for wide in WIDTHS],
        [((3, PIECE, wide), BF16) for wide in WIDTHS],
        [((PIECE, wide), BF16) for wide in WIDTHS[:RELAYED]],
        [((PIECE, wide), BF16) for wide in WIDTHS[:RELAYED]],
        [((2, PIECE, wide), F32) for wide in WIDTHS[:RELAYED]],
        ((PIECE, COLS), F32),
    ]
    outs = (small, small, small, shape((PIECE, COLS), F32), modal, modal)
    found = pl.pallas_call(
        body,
        out_shape=outs,
        in_specs=[pl.BlockSpec(memory_space=pl.ANY)] * 7,
        out_specs=(vmem,) * 6,
        scratch_shapes=[
            [pltpu.VMEM(*one) for one in entry] if isinstance(entry, list) else pltpu.VMEM(*entry)
            for entry in scratch
        ]
        + [
            pltpu.SemaphoreType.DMA((10,)),
            pltpu.SemaphoreType.DMA((SLOTS,)),
            pltpu.SemaphoreType.DMA((SLOTS,)),
        ],
        compiler_params=pltpu.CompilerParams(
            collective_id=0, has_side_effects=True, vmem_limit_bytes=56 * 2**20
        ),
        cost_estimate=pl.CostEstimate(
            flops=2 * 2**31, bytes_accessed=20 * 2**20, transcendentals=0
        ),
    )(query_act, key_act, value_act, grad_out, residue, decay_rate, out_weight)
    return pl.pallas_call(
        settle,
        out_shape=outs,
        in_specs=[vmem] * len(outs),
        out_specs=(vmem,) * len(outs),
    )(*found)


def solution(mesh):
    both = P("seq", "chan")
    chan = P(None, "chan")
    return jax.shard_map(
        per_device,
        mesh=mesh,
        in_specs=(both, both, both, chan, chan, chan, both),
        out_specs=(both, both, both, both, chan, chan),
        check_vma=False,
    )
```

time: 105 us -> 72 us (0.69)
  Pallas kernels: 93.3 us -> 71.2 us
  local copies, waits for them, and re-layouts: 10.3 us -> 0 us
    pallas_call x1 -> x2, Pallas kernels: 93.3 us -> 71.2 us  [the longest x1 68.5 us: per_device(): pl.pallas_call(body, out_shape=outs, in_specs=[pl.BlockSpec(memory_space=...]
    unnamed x6 -> x0, local copies, waits for them, and re-layouts: 10.3 us -> none
where the time goes in v3:
time: 72 us; the launch traced here: 71.9 us
  Pallas kernels  71.2 us (99%)
    pallas_call x1, Pallas kernels, per_device(): pl.pallas_call(body, out_shape=outs, in_specs=[pl.BlockSpec(memory_space=...  68.5 us
    pallas_call x1, Pallas kernels, per_device(): pl.pallas_call(settle, out_shape=outs, in_specs=[vmem] * len(outs), out_s...  2.71 us

profile of v3, /device:TPU:0, one launch (start us, length us, event | category | flops | bytes accessed | tf_op | source)
XLA Modules:
  0.0 71.9 jit_solution(11136940112667920028)
XLA Ops:
  0.6 68.5 %shard_map.118 = (bf16[128,1024]{1,0:T(8,128)(2,1)}, bf16[128,1024]{1,0:T(8,128)(2,1)}, bf16[128,1024]{1,0:T(8,128)(2,1)}, f32[256,1024]{1,0:T(8,128)}, f32[16,1024]{1,0:T(8,128)}, /*index=5*/f32[16,1024]{1,0:T(8,128)}) custom-call(bf16[128,1024]{1,0:T(8,128)(2,1)} %q_hbm.1, bf16[128,1024]{1,0:T(8,128)(2,1)} %k_hbm.1, bf16[128,1024]{1,0:T(8,128)(2,1)} %v_hbm.1, ...), custom_call_target="tpu_custom_call" | custom-call | flops 4294967296 | bytes 20971520 | tf_op jit(solution)/shard_map/pallas_call | solution.py:561
  69.2 2.7 %shard_map.119 = (bf16[128,1024]{1,0:T(8,128)(2,1)}, bf16[128,1024]{1,0:T(8,128)(2,1)}, bf16[128,1024]{1,0:T(8,128)(2,1)}, f32[256,1024]{1,0:T(8,128)}, f32[16,1024]{1,0:T(8,128)}, /*index=5*/f32[16,1024]{1,0:T(8,128)}) custom-call(bf16[128,1024]{1,0:T(8,128)(2,1)} %get-tuple-element.12.refs_0_, bf16[128,1024]{1,0:T(8,128)(2,1)} %get-tuple-element.13.refs_1_, ...), custom_call_target="tpu_custom_call" | custom-call | tf_op jit(solution)/shard_map/pallas_call | solution.py:582

commit v4 on v3

--- a/solution.py
+++ b/solution.py
@@ -17,9 +17,10 @@
 PARTS = 4
 DPART = 2048
 PIECE = 256
-WIDTHS = (256, 256, 256, 128, 128)
+WIDTHS = (128, 128, 128, 128, 128, 128, 128, 128)
+GROUPS = ((0, 1), (2, 3), (4, 5), (6,), (7,))
 CHUNKS = len(WIDTHS)
-RELAYED = 3
+RELAYED = 6
 DEPTH = 512
 
 
@@ -31,7 +32,7 @@
     q_hbm, k_hbm, v_hbm, g_hbm, res_hbm, rate_hbm, w_ref,
     gq_ref, gk_ref, gv_ref, gw_ref, gr_ref, gl_ref,
     q_ref, k_ref, v_ref, g_ref, res_ref, rate_ref,
-    wv, xs, cs, ys, hb, al, rl, gall, gt, turned, at, gat, gm, co,
+    wv, xs, cs, ys, hb, al, rl, gall, gt, zbuf, turned, at, gat, gm, co,
     hs, hin, so, sin, yin, gs, gin, yin2, to, tin, pq, pin, yp, pr, prin,
     rs_send, rs_recv, relay_send, relay_recv, held, own, wsem, ssem, rsem,
 ):
@@ -89,7 +90,8 @@
     barrier = pltpu.get_barrier_semaphore()
     greeted = [plane(k) for k in range(1, PLANE)] + [layer(k) for k in range(1, LAYERS)]
     greeted += [(s, sib), (s, far)]
-    greeted += [(y * PLANE + place(k, 1), far) for k in range(4)]
+    beside = y * PLANE + place(0, 1)
+    greeted.append((beside, far))
     for device in greeted:
         pl.semaphore_signal(barrier, inc=1, device_id=device, device_id_type=MESH)
 
@@ -177,22 +179,18 @@
     g_far, g_pass = {}, {}
     gall[c] = g_ref[...]
 
-    for k in range(PLANE):
-        gt[k] = g_ref[:, PIECE * k : PIECE * (k + 1)].T
+    for turn in range(2):
+        for k in range(4):
+            gt[turn, k] = g_ref[:, tile(place(k, turn), PIECE)].T
     a_slot = ids(16)
     mine = tile(p, ROWS)
+    z_in = [send(gt.at[1], zbuf.at[0], (beside, c), a_slot + 3)]
+    z_in.append(send(gt.at[1], zbuf.at[1], (beside, far), a_slot + 7))
     a_near = [
-        send(gt.at[place(k, 0)], at.at[c, :, mine], across(k), a_slot + k - 1) for k in range(1, 4)
+        send(gt.at[0, k], at.at[c, :, mine], across(k), a_slot + k - 1) for k in range(1, 4)
     ]
-    at[c, :, mine] = gt[p]
-    a_near += [
-        send(gt.at[place(k, 1)], at.at[c, :, mine], (y * PLANE + place(k, 1), c), a_slot + 3 + k)
-        for k in range(4)
-    ]
-    a_cross = [
-        send(gt.at[place(k, 1)], at.at[c, :, mine], (y * PLANE + place(k, 1), far), a_slot + 7 + k)
-        for k in range(4)
-    ]
+    at[c, :, mine] = gt[0, 0]
+    a_cross = []
     far_part(1)
 
     seen = set()
@@ -240,6 +238,14 @@
     s_in = to_owners(so, sin, 16)
     far_part(2)
     far_part(3)
+    beyond = tile(place(0, 1), ROWS)
+    for n, (h, found) in enumerate(((c, a_near), (far, a_cross))):
+        z_in[n].wait_recv()
+        at[h, :, beyond] = zbuf[n, 0]
+        found += [
+            send(zbuf.at[n, k], at.at[h, :, beyond], across(k), a_slot + 3 + 4 * n + k)
+            for k in range(1, 4)
+        ]
     far_pass(1)
 
     loads["q"].wait()
@@ -266,14 +272,22 @@
     distant = tile(place(2, 0), ROWS)
     gat_z, gat_x2, gat_in = [], [], []
 
-    def spread(chunk):
+    def spread(group):
+        for chunk in GROUPS[group]:
+            spread_one(chunk)
+
+    def spread_one(chunk):
         slot = gat_slot + chunk * (PLANE - 1)
         block = gat[chunk].at[mine]
         gat_z.append(send(block, block, (y * PLANE + other, c), slot))
         gat_x2.append(send(block, block, across(2), slot + 2))
         gat_in.append([send(block, block, across(k), slot + k) for k in (1, 3)])
 
-    def spread_more(chunk):
+    def spread_more(group):
+        for chunk in GROUPS[group]:
+            spread_more_one(chunk)
+
+    def spread_more_one(chunk):
         slot = gat_slot + chunk * (PLANE - 1) + 4
         block = gat[chunk].at[theirs]
         gat_z[chunk].wait_recv()
@@ -285,7 +299,7 @@
         gat_x2[chunk].wait_recv()
         gat_in[chunk].append(send(block, block, (y * PLANE + other, c), slot + 2))
 
-    straight = (0,)
+    straight = GROUPS[0]
     starts = [sum(WIDTHS[:n]) for n in range(CHUNKS)]
     for i in range(TILES):
         lanes = slice(128 * i, 128 * (i + 1))
@@ -295,7 +309,7 @@
         chunk = max(n for n in range(CHUNKS) if starts[n] <= 128 * i)
         from_lane = 128 * i - starts[chunk]
         gat[chunk][mine, from_lane : from_lane + 128] = gated
-        if 128 * (i + 1) == WIDTHS[0]:
+        if 128 * (i + 1) == sum(WIDTHS[n] for n in GROUPS[0]):
             spread(0)
 
     far_part(0)
@@ -365,7 +379,11 @@
     def partial(chunk, k):
         return jnp.dot(at[(y + k) % LAYERS], gat[chunk][...], preferred_element_type=F32)
 
-    def product(chunk):
+    def product(group):
+        for chunk in GROUPS[group]:
+            product_one(chunk)
+
+    def product_one(chunk):
         arrive(gat_in[chunk])
         slot = rs_slot + chunk * 3
         value = partial(chunk, 2).astype(BF16)
@@ -386,7 +404,11 @@
                 )
         own[:, starts[chunk] : starts[chunk] + WIDTHS[chunk]] = partial(chunk, 0)
 
-    def pass_on(chunk):
+    def pass_on(group):
+        for chunk in GROUPS[group]:
+            pass_on_one(chunk)
+
+    def pass_on_one(chunk):
         arrive(relay_in[chunk])
         for n, (k, added, alone) in enumerate(((1, top, low), (3, low, top))):
             value = held[chunk][n, added, :] + relay_recv[chunk][added, :].astype(F32)
@@ -500,7 +522,7 @@
         copy.wait_send()
 
 
-SLOTS = 160
+SLOTS = 192
 
 
 def settle(*refs):
@@ -529,7 +551,8 @@
         ((MODES * 8, 128), F32),
         ((MODES * 8, 128), F32),
         ((PARTS, ROWS, DPART), BF16),
-        ((PLANE, PIECE, ROWS), BF16),
+        ((2, 4, PIECE, ROWS), BF16),
+        ((2, 4, PIECE, ROWS), BF16),
         ((4, PIECE, ROWS), BF16),
         ((PARTS, PIECE, PLANE * ROWS), BF16),
         [((PLANE * ROWS, wide), BF16) for wide in WIDTHS],

time: 72 us -> 69.3 us (0.962)
  Pallas kernels: 71.2 us -> 68.5 us
    pallas_call x1, Pallas kernels: 68.5 us -> 65.8 us  [per_device(): pl.pallas_call(body, out_shape=outs, in_specs=[pl.BlockSpec(memory_space=...]
where the time goes in v4:
time: 69.3 us; the launch traced here: 69.2 us
  Pallas kernels  68.5 us (99%)
    pallas_call x1, Pallas kernels, per_device(): pl.pallas_call(body, out_shape=outs, in_specs=[pl.BlockSpec(memory_space=...  65.8 us
    pallas_call x1, Pallas kernels, per_device(): pl.pallas_call(settle, out_shape=outs, in_specs=[vmem] * len(outs), out_s...  2.71 us

profile of v4, /device:TPU:0, one launch (start us, length us, event | category | flops | bytes accessed | tf_op | source)
XLA Modules:
  0.0 69.2 jit_solution(5897553305445929826)
XLA Ops:
  0.6 65.8 %shard_map.118 = (bf16[128,1024]{1,0:T(8,128)(2,1)}, bf16[128,1024]{1,0:T(8,128)(2,1)}, bf16[128,1024]{1,0:T(8,128)(2,1)}, f32[256,1024]{1,0:T(8,128)}, f32[16,1024]{1,0:T(8,128)}, /*index=5*/f32[16,1024]{1,0:T(8,128)}) custom-call(bf16[128,1024]{1,0:T(8,128)(2,1)} %q_hbm.1, bf16[128,1024]{1,0:T(8,128)(2,1)} %k_hbm.1, bf16[128,1024]{1,0:T(8,128)(2,1)} %v_hbm.1, ...), custom_call_target="tpu_custom_call" | custom-call | flops 4294967296 | bytes 20971520 | tf_op jit(solution)/shard_map/pallas_call | solution.py:584
  66.5 2.7 %shard_map.119 = (bf16[128,1024]{1,0:T(8,128)(2,1)}, bf16[128,1024]{1,0:T(8,128)(2,1)}, bf16[128,1024]{1,0:T(8,128)(2,1)}, f32[256,1024]{1,0:T(8,128)}, f32[16,1024]{1,0:T(8,128)}, /*index=5*/f32[16,1024]{1,0:T(8,128)}) custom-call(bf16[128,1024]{1,0:T(8,128)(2,1)} %get-tuple-element.12.refs_0_, bf16[128,1024]{1,0:T(8,128)(2,1)} %get-tuple-element.13.refs_1_, ...), custom_call_target="tpu_custom_call" | custom-call | tf_op jit(solution)/shard_map/pallas_call | solution.py:605

commit v5 on v4

--- a/solution.py
+++ b/solution.py
@@ -350,6 +350,7 @@
     spread(2)
     spread_more(1)
     spread(3)
+    spread(4)
 
     half = MODES // 2
     for part in range(2):
@@ -418,10 +419,10 @@
                 send(rs_send[chunk].at[n], rs_recv[chunk].at[n], layer(k), rs_slot + chunk * 3 + n)
             )
 
+    spread_more(2)
     arrive(a_sib)
     product(0)
-    spread_more(2)
-    spread(4)
+    spread_more(3)
 
     arrive(g_in)
     state = blank
@@ -444,7 +445,7 @@
 
     pass_on(0)
     product(1)
-    spread_more(3)
+    spread_more(4)
 
     arrive(y2_in)
     after, chosen = blank, blank
@@ -458,7 +459,6 @@
     p_in = to_owners(pq, pin, 48)
     pass_on(1)
     product(2)
-    spread_more(4)
 
     arrive(p_in)
     plain, ramp = blank, blank

time: 69.3 us -> 72.5 us (1.046); the launches traced: 69.2 us -> 71.5 us
  Pallas kernels: 68.5 us -> 70.8 us
    pallas_call x1, Pallas kernels: 65.8 us -> 68.1 us  [per_device(): pl.pallas_call(body, out_shape=outs, in_specs=[pl.BlockSpec(memory_space=...]
where the time goes in v5:
time: 72.5 us; the launch traced here: 71.5 us
  Pallas kernels  70.8 us (98%)
    pallas_call x1, Pallas kernels, per_device(): pl.pallas_call(body, out_shape=outs, in_specs=[pl.BlockSpec(memory_space=...  68.1 us
    pallas_call x1, Pallas kernels, per_device(): pl.pallas_call(settle, out_shape=outs, in_specs=[vmem] * len(outs), out_s...  2.71 us

profile of v5, /device:TPU:0, one launch (start us, length us, event | category | flops | bytes accessed | tf_op | source)
XLA Modules:
  0.0 71.5 jit_solution(9616789434620465104)
XLA Ops:
  0.6 68.1 %shard_map.118 = (bf16[128,1024]{1,0:T(8,128)(2,1)}, bf16[128,1024]{1,0:T(8,128)(2,1)}, bf16[128,1024]{1,0:T(8,128)(2,1)}, f32[256,1024]{1,0:T(8,128)}, f32[16,1024]{1,0:T(8,128)}, /*index=5*/f32[16,1024]{1,0:T(8,128)}) custom-call(bf16[128,1024]{1,0:T(8,128)(2,1)} %q_hbm.1, bf16[128,1024]{1,0:T(8,128)(2,1)} %k_hbm.1, bf16[128,1024]{1,0:T(8,128)(2,1)} %v_hbm.1, ...), custom_call_target="tpu_custom_call" | custom-call | flops 4294967296 | bytes 20971520 | tf_op jit(solution)/shard_map/pallas_call | solution.py:584
  68.8 2.7 %shard_map.119 = (bf16[128,1024]{1,0:T(8,128)(2,1)}, bf16[128,1024]{1,0:T(8,128)(2,1)}, bf16[128,1024]{1,0:T(8,128)(2,1)}, f32[256,1024]{1,0:T(8,128)}, f32[16,1024]{1,0:T(8,128)}, /*index=5*/f32[16,1024]{1,0:T(8,128)}) custom-call(bf16[128,1024]{1,0:T(8,128)(2,1)} %get-tuple-element.12.refs_0_, bf16[128,1024]{1,0:T(8,128)(2,1)} %get-tuple-element.13.refs_1_, ...), custom_call_target="tpu_custom_call" | custom-call | tf_op jit(solution)/shard_map/pallas_call | solution.py:605
